TPU v7x, 256 devices: a whole 4x4x8 slice. The times are simulated.
256 devices in a mesh: gx: 8 (over z), gy: 4 (over x), gz: 8 (over y, core).
Axes of the slice: x: 4, y: 4, z: 8, core: 2. Of those that a mesh axis runs over, the one named last changes fastest.
Arguments:
- right_side: float32 [256, 64, 1024], P('gx', 'gy', 'gz'), may hold values from -4 to 4
- phase_mask: int32 [256, 64, 1024], P('gx', 'gy', 'gz'), may hold values 0 or 1
Outputs:
- pressure: float32 [256, 64, 1024], P('gx', 'gy', 'gz')
- residual: float32 [256, 64, 1024], P('gx', 'gy', 'gz')
All inputs are finite; a program needn't handle non-finite values. No bound on the sum of `phase_mask` on one device may be relied on, other than what follows from the above.
Results may differ from a plain program's by a relative error of at most 0.0003.
Values sent between devices are 32-bit elements; how exact they have to be, the bound alone decides.
No kernel may reach another device: no remote copies, remote signals or barrier semaphores. Data moves between devices by JAX's collectives and lax.ppermute only.
A program may use at most 192 MiB of HBM per device.

v0:
```python
import functools

import jax
import jax.numpy as jnp
from jax import lax
from jax.experimental import pallas as pl
from jax.experimental.pallas import tpu as pltpu
from jax.sharding import PartitionSpec as P

COARSE_ITERS = 8
SMOOTH_LOW = 0.25
SMOOTH_HIGH = 2.0
COARSE_LOW = 0.02
LIQUID = 10.0
GAS = 1.0

INTERPRET = False
VMEM_LIMIT = 40 * 1024 * 1024

BX, BY, BZ = 32, 16, 128
WX = 8
X0, Y0, Z0 = BX + 2 * WX, 32, 256
X1, Y1G, Z1 = 48, 8, 128
X2 = 24
F32 = jnp.float32


def chebyshev(low, degree):
    theta = 0.5 * (SMOOTH_HIGH + low)
    delta = 0.5 * (SMOOTH_HIGH - low)
    sigma = theta / delta
    rho_old = 1.0 / sigma
    steps = []
    for _ in range(1, degree):
        rho_new = 1.0 / (2.0 * sigma - rho_old)
        steps.append((rho_new * rho_old, 2.0 * rho_new / delta))
        rho_old = rho_new
    return 1.0 / theta, steps


FIRST, ((KEEP, GAIN),) = chebyshev(SMOOTH_LOW, 2)
COARSE_FIRST, COARSE_STEPS = chebyshev(COARSE_LOW, COARSE_ITERS)


def roll(values, shift, axis):
    return pltpu.roll(values, shift % values.shape[axis], axis)


def iota(shape, dim):
    return lax.broadcasted_iota(jnp.int32, shape, dim)


def dot(left, right):
    return jnp.dot(left, right, precision=lax.Precision.HIGHEST, preferred_element_type=F32)


def lane_pairs(fine, weight, odd_only=False):
    z = iota((fine, 128), 0)
    half = z >> 1
    if fine == 128:
        half = jnp.where(z >= 96, half + 64, half)
    hit = half == iota((fine, 128), 1)
    if odd_only:
        hit = hit & ((z & 1) == 1)
    return jnp.where(hit, weight, 0.0).astype(F32)


def lane_copies(fine):
    z = iota((128, fine), 1)
    half = z >> 1
    if fine == 128:
        half = jnp.where(z >= 96, half + 64, half)
    return jnp.where(half == iota((128, fine), 0), 1.0, 0.0).astype(F32)


def row_pairs(rows, odd_x=False, odd_y=False):
    shape = (2 * rows, 8 * rows)
    shift = rows.bit_length() - 1
    c, f = iota(shape, 0), iota(shape, 1)
    cx, cy = c >> (shift - 1), c & (rows // 2 - 1)
    x, y = f >> shift, f & (rows - 1)
    hit = ((x >> 1) == cx) & ((y >> 1) == cy)
    if odd_x:
        hit = hit & ((x & 1) == 1)
    if odd_y:
        hit = hit & ((y & 1) == 1)
    return jnp.where(hit, 1.0, 0.0).astype(F32)


def row_copies(rows):
    shape = (8 * rows, 2 * rows)
    shift = rows.bit_length() - 1
    f, c = iota(shape, 0), iota(shape, 1)
    hit = ((f >> (shift + 1)) == (c >> (shift - 1))) & (((f & (rows - 1)) >> 1) == (c & (rows // 2 - 1)))
    return jnp.where(hit, 1.0, 0.0).astype(F32)


def coarsen(block, rows_matrix, lanes_matrix):
    planes, rows, lanes = block.shape
    out = dot(dot(rows_matrix, block.reshape(planes * rows, lanes)), lanes_matrix)
    return out.reshape(4, rows // 2, 128)


def refine(block, rows_matrix, lanes_matrix):
    planes, rows, lanes = block.shape
    out = dot(rows_matrix, dot(block.reshape(planes * rows, lanes), lanes_matrix))
    return out.reshape(8, 2 * rows, lanes_matrix.shape[1])


def apply_at(v, at, planes, faces):
    fx, fy, fz, diag = faces
    here = pl.ds(at, planes)
    c = v[here]
    y, z = fy[here], fz[here]
    out = diag[here] * c - fx[here] * v[pl.ds(at + 1, planes)] - fx[pl.ds(at - 1, planes)] * v[pl.ds(at - 1, planes)]
    out = out - y * roll(c, -1, 1) - roll(y * c, 1, 1)
    return out - z * roll(c, -1, 2) - roll(z * c, 1, 2)


def step_x(values, by):
    if by > 0:
        return jnp.concatenate([values[-1:], values[:-1]], 0)
    return jnp.concatenate([values[1:], values[:1]], 0)


def apply_to(v, faces):
    fx, fy, fz, diag = faces
    out = diag * v - fx * step_x(v, -1) - step_x(fx * v, 1)
    out = out - fy * roll(v, -1, 1) - roll(fy * v, 1, 1)
    return out - fz * roll(v, -1, 2) - roll(fz * v, 1, 2)


def inverse(diag):
    return 1.0 / jnp.where(diag > 0.0, diag, 1.0)


def level_of(fx, fx_before, fy, fz, gx, gy, gz, sizes):
    nx, ny, nz = sizes
    diag = fx + jnp.where(gx == 0, 0.0, fx_before)
    diag = diag + fy + jnp.where(gy == 0, 0.0, roll(fy, 1, 1))
    diag = diag + fz + jnp.where(gz == 0, 0.0, roll(fz, 1, 2))
    fx = jnp.where((gx == nx - 1) | (gx == -1), 0.0, fx)
    fy = jnp.where((gy == ny - 1) | (gy == -1), 0.0, fy)
    fz = jnp.where((gz == nz - 1) | (gz == -1), 0.0, fz)
    return fx, fy, fz, diag, inverse(diag)


def loop(start, stop, block, body):
    count = (stop - start) // block
    assert count * block == stop - start

    def step(i, carry):
        body(start + i * block)
        return carry

    lax.fori_loop(0, count, step, 0)


def send_z(r, mask, to_upper, to_lower):
    density = GAS + (LIQUID - GAS) * mask[...].astype(F32)
    turned = roll(density, 64, 2)
    lane = iota(density.shape, 2)
    to_upper[...] = jnp.where(lane >= 64, r[...], turned)
    to_lower[...] = jnp.where(lane < 64, r[...], turned)


def send_y(r, mask, below, above, to_upper, to_lower):
    density = GAS + (LIQUID - GAS) * mask[...].astype(F32)
    low, high = below[...], above[...]
    lane = iota(density.shape, 2)
    r_side = jnp.where(lane < 64, high, low)
    d_side = roll(jnp.where(lane >= 64, high, low), 64, 2)
    for out, rows, line in ((to_upper, slice(8, 16), 7), (to_lower, slice(0, 8), 8)):
        out[0:BX, :, 0:128] = r[:, rows, :]
        out[0:BX, :, 128:256] = r_side[:, rows]
        out[BX : 2 * BX, :, 0:128] = density[:, rows]
        out[BX : 2 * BX, :, 128:256] = d_side[:, rows]
        for x in range(BX):
            at = 2 * BX + x // 8
            out[at, x % 8 : x % 8 + 1, 0:128] = density[x, line : line + 1]
            out[at, x % 8 : x % 8 + 1, 128:256] = d_side[x, line : line + 1]


def send_x(lower, upper, below, above, to_upper, to_lower):
    for out, r_at, d_at, pack in ((to_upper, BX - 8, BX - 9, 3), (to_lower, 0, 0, 0)):
        for tile, source in enumerate((lower, upper, above, below)):
            rows = slice(8 * tile, 8 * tile + 8)
            out[0:8, rows] = source[r_at : r_at + 8]
            out[8:17, rows] = source[BX + d_at : BX + d_at + 9]
        out[17, 0:8] = below[2 * BX + pack]
        out[17, 8:16] = above[2 * BX + pack]
        out[17, 16:32] = jnp.zeros((16, Z0), F32)


def presmooth_0(where, r, faces, inv, d0, d1, start, stop, have_first):
    if not have_first:
        def first(at):
            here = pl.ds(at, 2)
            d0[here] = (FIRST * r[here]) * inv[here]

        loop(start, stop, 2, first)

    def second(at):
        here = pl.ds(at, 2)
        left = r[here] - apply_at(d0, at, 2, faces)
        r[here] = left
        d1[here] = KEEP * d0[here] + GAIN * (left * inv[here])

    loop(start + 1, stop - 1, 2, second)

    def third(at):
        here = pl.ds(at, 2)
        r[here] = r[here] - apply_at(d1, at, 2, faces)

    loop(start + 2, stop - 2, 2, third)


def restrict_0(r, out):
    rows, lanes = row_pairs(16), lane_pairs(256, 0.125)
    for g in range(4):
        block = r[WX + 8 * g : WX + 8 * g + 8, 0:16, :]
        out[4 * g : 4 * g + 4] = coarsen(block, rows, lanes)


def add_own(total, terms, first):
    value = None if first else total[...]
    for term in terms:
        own = term[WX : WX + BX, 0:BY, 0:BZ]
        value = own if value is None else value + own
    total[...] = value


def begin(sizes, where, lower, upper, below, above, x_below, x_above,
          fx, fy, fz, diag, inv, r, total, packed, rho, low, up, raw_x, raw_y, raw_z, d0, d1):
    nx, ny, nz = sizes
    gx0, gy0, gz0 = where[0] * BX, where[1] * BY, where[2] * BZ
    r[0:8] = x_below[0:8]
    r[40:48] = x_above[0:8]
    rho[0:9] = x_below[8:17]
    rho[41:50] = x_above[8:17]
    for tile, source in enumerate((lower, upper, above, below)):
        rows = slice(8 * tile, 8 * tile + 8)
        r[8:40, rows] = source[0:BX]
        rho[9:41, rows] = source[BX : 2 * BX]
    low[0:8] = x_below[17, 0:8]
    up[0:8] = x_below[17, 8:16]
    low[40:48] = x_above[17, 0:8]
    up[40:48] = x_above[17, 8:16]
    low[8:40] = below[2 * BX : 2 * BX + 4].reshape(BX, Z0)
    up[8:40] = above[2 * BX : 2 * BX + 4].reshape(BX, Z0)

    def plane(p):
        shape = (Y0, Z0)
        row, lane = iota(shape, 0), iota(shape, 1)
        gy = gy0 + jnp.where(row < 24, row, row - 32)
        gz = gz0 + jnp.where(lane < 192, lane, lane - 256)
        gx = gx0 + p - WX
        c = rho[p + 1]
        f_x = 2.0 / (c + jnp.where(gx == nx - 1, GAS, rho[p + 2]))
        l_x = jnp.where(gx == 0, 0.0, 2.0 / (c + rho[p]))
        over = jnp.where(row == 23, up[pl.ds(p, 1)], roll(c, -1, 0))
        under = jnp.where(row == 24, low[pl.ds(p, 1)], roll(c, 1, 0))
        f_y = 2.0 / (c + jnp.where(gy == ny - 1, GAS, over))
        l_y = jnp.where(gy == 0, 0.0, 2.0 / (c + under))
        f_z = 2.0 / (c + jnp.where(gz == nz - 1, GAS, roll(c, -1, 1)))
        l_z = jnp.where(gz == 0, 0.0, roll(f_z, 1, 1))
        d = f_x + l_x + f_y + l_y + f_z + l_z
        i = 1.0 / d
        diag[p] = d
        inv[p] = i
        d0[p] = (FIRST * r[p]) * i
        raw_x[p] = f_x[0:16]
        raw_y[p] = f_y[0:16]
        raw_z[p] = f_z[0:16]
        fx[p] = jnp.where((gx == nx - 1) | (gx == -1), 0.0, f_x)
        fy[p] = jnp.where((gy == ny - 1) | (gy == -1), 0.0, f_y)
        fz[p] = jnp.where((gz == nz - 1) | (gz == -1), 0.0, f_z)

    loop(0, X0, 1, plane)
    faces = (fx, fy, fz, diag)
    presmooth_0(where, r, faces, inv, d0, d1, 0, X0, True)
    add_own(total, (d0, d1), True)
    restrict_0(r, packed.at[0:16])
    lanes, odd_lanes = lane_pairs(256, 0.125), lane_pairs(256, 0.125, True)
    for n, (raw, rows, columns) in enumerate((
        (raw_x, row_pairs(16, odd_x=True), lanes),
        (raw_y, row_pairs(16, odd_y=True), lanes),
        (raw_z, row_pairs(16), odd_lanes),
    )):
        for g in range(4):
            block = raw[WX + 8 * g : WX + 8 * g + 8]
            packed[16 * (n + 1) + 4 * g : 16 * (n + 1) + 4 * g + 4] = coarsen(block, rows, columns)


def assemble_1(part, own, below, above, out):
    out[0:16] = below[part]
    out[16:32] = own[part]
    out[32:48] = above[part]


def relax_1(r, faces, inv, d0, d1, start, stop):
    def second(at):
        here = pl.ds(at, 2)
        left = r[here] - apply_at(d0, at, 2, faces)
        r[here] = left
        d1[here] = KEEP * d0[here] + GAIN * (left * inv[here])

    loop(start, stop, 2, second)


def down(sizes, first, where, own, below, above, *refs):
    n1 = tuple(n // 2 for n in sizes)
    n2 = tuple(n // 4 for n in sizes)
    if first:
        (fx, fy, fz, diag, inv, gx2, gy2, gz2, diag2, inv2, r, e, r2_out, e2_out, packed, d0, d1) = refs
    else:
        (fx, fy, fz, diag, inv, gx2, gy2, gz2, diag2, inv2, r, e, r2_out, e2_out, packed, d0, d1) = refs
    ny1 = fx.shape[1]
    ny2 = ny1 // 2
    assemble_1(slice(0, 16), own, below, above, r)
    rows, lanes = row_pairs(ny1), lane_pairs(128, 0.125)
    if first:
        raws = (fx, fy, fz)
        for n, raw in enumerate(raws):
            assemble_1(slice(16 * (n + 1), 16 * (n + 2)), own, below, above, raw)
        odd_lanes = lane_pairs(128, 0.125, True)
        coarse = []
        for raw, rows_matrix, columns in (
            (fx, row_pairs(ny1, odd_x=True), lanes),
            (fy, row_pairs(ny1, odd_y=True), lanes),
            (fz, rows, odd_lanes),
        ):
            coarse.append(jnp.concatenate(
                [coarsen(raw[8 * g : 8 * g + 8], rows_matrix, columns) for g in range(6)], 0))
        shape = (2, ny1, 128)
        gy = lax.rem(where[1] * 8 + iota(shape, 1), n1[1])
        lane = iota(shape, 2)
        gz = where[2] * 64 + jnp.where(lane < 96, lane, lane - 128)

        def planes(n):
            at = X1 - 2 - n
            here = pl.ds(at, 2)
            gx = where[0] * 16 + at - 16 + iota(shape, 0)
            before = jnp.concatenate([fx[pl.ds(jnp.maximum(at - 1, 0), 1)], fx[pl.ds(at, 1)]], 0)
            level = level_of(fx[here], before, fy[here], fz[here], gx, gy, gz, n1)
            fx[here], fy[here], fz[here], diag[here], inv[here] = level
            d0[here] = (FIRST * r[here]) * level[4]

        loop(0, X1, 2, planes)
        shape = (X2, ny2, 128)
        lane = iota(shape, 2)
        at_2 = (
            where[0] * 8 - 8 + iota(shape, 0),
            lax.rem(where[1] * 4 + iota(shape, 1), n2[1]),
            where[2] * 32 + jnp.where(lane < 64, lane, lane - 128),
        )
        raw_2 = tuple(coarse)
        level_2 = level_of(raw_2[0], step_x(raw_2[0], 1), raw_2[1], raw_2[2], *at_2, n2)
        gx2[...], gy2[...], gz2[...], diag2[...], inv2[...] = level_2
        for n, (rows_matrix, columns) in enumerate((
            (row_pairs(ny2, odd_x=True), lanes),
            (row_pairs(ny2, odd_y=True), lanes),
            (row_pairs(ny2), odd_lanes),
        )):
            packed[4 * (n + 1) : 4 * (n + 2)] = coarsen(raw_2[n][8:16], rows_matrix, columns)
    else:
        def begin_1(at):
            here = pl.ds(at, 2)
            d0[here] = (FIRST * r[here]) * inv[here]

        loop(0, X1, 2, begin_1)

    faces = (fx, fy, fz, diag)
    relax_1(r, faces, inv, d0, d1, 1, X1 - 1)

    def third(at):
        here = pl.ds(at, 2)
        r[here] = r[here] - apply_at(d1, at, 2, faces)
        e[here] = d0[here] + d1[here]

    loop(2, X1 - 2, 2, third)
    e[0:2] = d0[0:2]
    e[X1 - 2 : X1] = d0[X1 - 2 : X1]
    r2 = jnp.concatenate([coarsen(r[8 * g : 8 * g + 8], rows, lanes) for g in range(6)], 0)
    faces_2 = (gx2[...], gy2[...], gz2[...], diag2[...])
    d = (FIRST * r2) * inv2[...]
    r2 = r2 - apply_to(d, faces_2)
    d_next = KEEP * d + GAIN * (r2 * inv2[...])
    r2 = r2 - apply_to(d_next, faces_2)
    r2_out[...] = r2
    e2_out[...] = d + d_next
    packed[0:4] = coarsen(r2[8:16], row_pairs(ny2), lanes)


def spread(own, below, above, out):
    lane = iota(own.shape, 2)
    values = jnp.where(lane < 16, own[...], 0.0)
    values = jnp.where((lane >= 16) & (lane < 32), roll(above[...], 16, 2), values)
    values = jnp.where(lane >= 112, roll(below[...], 112, 2), values)
    for d in range(out.shape[0]):
        out[d] = values


def up(sizes, last, where, gathered, *refs):
    n3 = tuple(n // 8 for n in sizes)
    first = not last
    refs = list(refs)
    take = lambda n: [refs.pop(0) for _ in range(n)]
    if last:
        level_3 = take(5)
    gx2, gy2, gz2, diag2, inv2, r2_in, e2_in = take(7)
    fx1, fy1, fz1, diag1, inv1, r1_in, e1_in = take(7)
    fx, fy, fz, diag, inv, r_in, total_in = take(7)
    if first:
        level_3 = take(5)
        r, total, packed = take(3)
    else:
        pressure, residual = take(2)
        (r,) = take(1)
    e3, p1, r1, a1, b1, c1, p0, d0, d1 = take(9)

    count = gathered.shape[0]
    ny3 = gathered.shape[2]
    shape = (4 * count, ny3, 128)
    r3 = gathered[:, 0:4].reshape(shape)
    if first:
        raw = [gathered[:, 4 * n : 4 * n + 4].reshape(shape) for n in (1, 2, 3)]
        lane = iota(shape, 2)
        at = (
            iota(shape, 0),
            lax.rem(where[1] * 2 + iota(shape, 1), n3[1]),
            where[2] * 16 + jnp.where(lane < 64, lane, lane - 128),
        )
        values = level_of(raw[0], step_x(raw[0], 1), raw[1], raw[2], *at, n3)
        for ref, value in zip(level_3, values):
            ref[...] = value
    faces = tuple(ref[...] for ref in level_3[:4])
    inv3 = level_3[4][...]
    d = (COARSE_FIRST * r3) * inv3
    total3 = d
    for keep, gain in COARSE_STEPS:
        r3 = r3 - apply_to(d, faces)
        d = keep * d + gain * (r3 * inv3)
        total3 = total3 + d
    e3[...] = total3

    copies_rows, copies_lanes = row_copies(2 * ny3), lane_copies(128)
    blocks = []
    for g in range(3):
        start = lax.rem(where[0] * 4 + 4 * (g - 1) + 4 * count, 4 * count)
        blocks.append(refine(e3[pl.ds(start, 4)], copies_rows, copies_lanes))
    p = jnp.concatenate(blocks, 0)
    faces = (gx2[...], gy2[...], gz2[...], diag2[...])
    r2 = r2_in[...] - apply_to(p, faces)
    d = (FIRST * r2) * inv2[...]
    r2 = r2 - apply_to(d, faces)
    d_next = KEEP * d + GAIN * (r2 * inv2[...])
    e2 = e2_in[...] + p + d + d_next

    copies_rows = row_copies(4 * ny3)
    for g in range(4):
        p1[8 + 8 * g : 16 + 8 * g] = refine(e2[4 + 4 * g : 8 + 4 * g], copies_rows, copies_lanes)
    faces = (fx1, fy1, fz1, diag1)

    def lift_1(at):
        here = pl.ds(at, 2)
        left = r1_in[here] - apply_at(p1, at, 2, faces)
        r1[here] = left
        a1[here] = (FIRST * left) * inv1[here]

    loop(11, 37, 2, lift_1)
    relax_1(r1, faces, inv1, a1, b1, 12, 36)

    def sum_1(at):
        here = pl.ds(at, 4)
        value = e1_in[here] + p1[here] + a1[here] + b1[here]
        c1[here, 0:8] = value[:, 0:8]
        tile = (4, 8, 128)
        c1[here, 8:16] = jnp.where(iota(tile, 1) < 4, value[:, 8:16], value[:, -8:])

    loop(12, 36, 4, sum_1)

    copies_rows, copies_lanes = row_copies(32), lane_copies(256)
    for g in range(6):
        p0[8 * g : 8 * g + 8] = refine(c1[12 + 4 * g : 16 + 4 * g], copies_rows, copies_lanes)
    faces = (fx, fy, fz, diag)
    begin_at, end_at = (6, 42) if last else (2, 46)

    def lift_0(at):
        here = pl.ds(at, 2)
        left = r_in[here] - apply_at(p0, at, 2, faces)
        r[here] = left
        d0[here] = (FIRST * left) * inv[here]

    loop(begin_at, end_at, 2, lift_0)
    presmooth_0(where, r, faces, inv, d0, d1, begin_at, end_at, True)
    if last:
        pressure[...] = total_in[...]
        add_own(pressure, (p0, d0, d1), False)
        residual[...] = r[WX : WX + BX, 0:BY, 0:BZ]
        return
    total[...] = total_in[...]
    add_own(total, (p0, d0, d1), False)
    presmooth_0(where, r, faces, inv, d0, d1, 4, 44, False)
    add_own(total, (d0, d1), False)
    restrict_0(r, packed)


def call(kernel, name, args, outs, scratch=()):
    vmem = pl.BlockSpec(memory_space=pltpu.VMEM)
    smem = pl.BlockSpec(memory_space=pltpu.SMEM)
    return pl.pallas_call(
        kernel,
        out_shape=[jax.ShapeDtypeStruct(s, F32) for s in outs],
        in_specs=[smem if a.ndim == 1 else vmem for a in args],
        out_specs=[vmem] * len(outs),
        scratch_shapes=[pltpu.VMEM(s, F32) for s in scratch],
        compiler_params=pltpu.CompilerParams(vmem_limit_bytes=VMEM_LIMIT),
        name=name,
        interpret=INTERPRET,
    )(*args)


def from_below(array, axis):
    n = lax.axis_size(axis)
    return lax.ppermute(array, axis, [(i, (i + 1) % n) for i in range(n)])


def from_above(array, axis, by=1):
    n = lax.axis_size(axis)
    return lax.ppermute(array, axis, [((i + by) % n, i) for i in range(n)])


def body(right_side, phase_mask):
    nx, ny, nz = (lax.axis_size(a) for a in ("gx", "gy", "gz"))
    sizes = (nx * BX, ny * BY, nz * BZ)
    where = jnp.stack([lax.axis_index(a) for a in ("gx", "gy", "gz")]).astype(jnp.int32)
    own = (BX, BY, BZ)
    to_upper, to_lower = call(send_z, "send_z", (right_side, phase_mask), [own] * 2)
    below, above = from_below(to_upper, "gz"), from_above(to_lower, "gz")
    part = (2 * BX + 4, 8, Z0)
    upper, lower = call(send_y, "send_y", (right_side, phase_mask, below, above), [part] * 2)
    below, above = from_below(upper, "gy"), from_above(lower, "gy")
    to_upper, to_lower = call(send_x, "send_x", (lower, upper, below, above), [(18, Y0, Z0)] * 2)
    x_below, x_above = from_below(to_upper, "gx"), from_above(to_lower, "gx")

    full = (X0, Y0, Z0)
    *faces_0, r0, total, packed = call(
        functools.partial(begin, sizes), "begin",
        (where, lower, upper, below, above, x_below, x_above),
        [full] * 6 + [own, (64, 8, 128)],
        [(X0 + 2, Y0, Z0), (X0, Z0), (X0, Z0)] + [(X0, BY, Z0)] * 3 + [full] * 2,
    )
    full_1 = (X1, 8 * ny, 128)
    full_2 = (X2, 4 * ny, 128)
    levels = []
    level_3 = []
    for cycle in range(2):
        first = cycle == 0
        parts = [packed] + [from_above(packed, "gy", s) for s in range(1, ny)]
        rows = jnp.concatenate(parts, 1)
        below, above = from_below(rows, "gx"), from_above(rows, "gx")
        state = [full_1] * 2 + [full_2] * 2
        planes = 16 if first else 4
        made = call(
            functools.partial(down, sizes, first), "down",
            (where, rows, below, above, *levels),
            ([full_1] * 5 + [full_2] * 5 if first else []) + state + [(planes, 2 * ny, 128)],
            [full_1] * 2,
        )
        if first:
            levels, made = made[:10], made[10:]
        r1, e1, r2, e2, packed = made
        below, above = from_below(packed, "gz"), from_above(packed, "gz")
        (copies,) = call(spread, "spread", (packed, below, above), [(nx,) + packed.shape])
        gathered = lax.all_to_all(copies, "gx", 0, 0)
        args = (where, gathered, *level_3, *levels[5:], r2, e2, *levels[:5], r1, e1, *faces_0, r0, total)
        full_3 = (4 * nx, 2 * ny, 128)
        scratch = [full_3] + [full_1] * 4 + [(X1, 16, 128)] + [full] * 3
        if first:
            *level_3, r0, total, packed = call(
                functools.partial(up, sizes, False), "up", args,
                [full_3] * 5 + [full, own, (16, 8, 128)], scratch)
        else:
            return tuple(call(functools.partial(up, sizes, True), "up_last", args, [own] * 2, [full] + scratch))


def solution(mesh):
    spec = P("gx", "gy", "gz")
    return jax.shard_map(body, mesh=mesh, in_specs=(spec, spec), out_specs=(spec, spec), check_vma=False)
```

profile of v0, /device:TPU:6, one launch (start us, length us, event | category | flops | bytes accessed | tf_op | source)
XLA Modules:
  0.0 226.9 jit_solution(16972730898757289661)
XLA Ops:
  0.6 0.0 copy-start.7
  0.6 0.9 copy-done.7
  1.6 0.9 copy-done.8
  2.5 0.1 send_z.1
  2.7 0.0 collective-permute-start
  2.7 2.9 %collective-permute-start.1 = (f32[32,16,128]{2,1,0:T(8,128)S(1)}, f32[32,16,128]{2,1,0:T(8,128)S(1)}, u32[]{:S(2)}, u32[]{:S(2)}) collective-permute-start(f32[32,16,128]{2,1,0:T(8,128)S(1)} %get-tuple-element.45), channel_id=1, source_target_pairs={{1,0},{2,1},{3,2},{4,3},{5,4},{6,5},{7,6},{0,7},{9,8},{10,9},{11,1... | collective-permute-start | bytes 786440 | tf_op jit(solution)/shard_map/ppermute | solution.py:531
  5.6 4.1 %collective-permute-done.below = f32[32,16,128]{2,1,0:T(8,128)S(1)} collective-permute-done((f32[32,16,128]{2,1,0:T(8,128)S(1)}, f32[32,16,128]{2,1,0:T(8,128)S(1)}, u32[]{:S(2)}, u32[]{:S(2)}) %collective-permute-start) | collective-permute-done | bytes 262176 | tf_op jit(solution)/shard_map/ppermute | solution.py:526
  9.7 0.0 collective-permute-done.1.above
  9.7 0.2 send_y.1
  9.9 0.9 collective-permute-start.3
  10.8 2.4 %collective-permute-start.2 = (f32[68,8,256]{2,1,0:T(8,128)S(1)}, f32[68,8,256]{2,1,0:T(8,128)S(1)}, u32[]{:S(2)}, u32[]{:S(2)}) collective-permute-start(f32[68,8,256]{2,1,0:T(8,128)S(1)} %get-tuple-element.47.upper), channel_id=1, source_target_pairs={{0,8},{8,16},{16,24},{24,0},{1,9},{9,17},{17,25},{25,1},{2,10},{10... | collective-permute-start | bytes 1671176 | tf_op jit(solution)/shard_map/ppermute | solution.py:526
  13.2 13.0 %collective-permute-done.3.above = f32[68,8,256]{2,1,0:T(8,128)S(1)} collective-permute-done((f32[68,8,256]{2,1,0:T(8,128)S(1)}, f32[68,8,256]{2,1,0:T(8,128)S(1)}, u32[]{:S(2)}, u32[]{:S(2)}) %collective-permute-start.3) | collective-permute-done | bytes 557088 | tf_op jit(solution)/shard_map/ppermute | solution.py:531
  26.2 0.0 collective-permute-done.2.below
  26.2 1.1 send_x.1
  27.3 1.9 collective-permute-start.4
  29.2 3.9 %collective-permute-start.5 = (f32[18,32,256]{2,1,0:T(8,128)}, f32[18,32,256]{2,1,0:T(8,128)S(1)}, u32[]{:S(2)}, u32[]{:S(2)}) collective-permute-start(f32[18,32,256]{2,1,0:T(8,128)} %get-tuple-element.49), channel_id=1, source_target_pairs={{32,0},{64,32},{96,64},{128,96},{160,128},{192,160},{224,192},{0,2... | collective-permute-start | bytes 1769480 | tf_op jit(solution)/shard_map/ppermute | solution.py:531
  33.1 0.1 pad_add_fusion.where
  33.2 13.3 %collective-permute-done.4.x_below = f32[18,32,256]{2,1,0:T(8,128)S(1)} collective-permute-done((f32[18,32,256]{2,1,0:T(8,128)}, f32[18,32,256]{2,1,0:T(8,128)S(1)}, u32[]{:S(2)}, u32[]{:S(2)}) %collective-permute-start.4) | collective-permute-done | bytes 589856 | tf_op jit(solution)/shard_map/ppermute | solution.py:526
  46.5 0.0 collective-permute-done.5.x_above
  46.5 16.0 %begin.1 = (f32[48,32,256]{2,1,0:T(8,128)S(1)}, f32[48,32,256]{2,1,0:T(8,128)S(1)}, f32[48,32,256]{2,1,0:T(8,128)S(1)}, f32[48,32,256]{2,1,0:T(8,128)S(1)}, f32[...) custom-call(s32[3]{0:T(128)S(1)} %pad_add_fusion.where, ...), custom_call_target="tpu_custom_call" | custom-call | tf_op jit(solution)/shard_map/begin/pallas_call | solution.py:512
  62.5 0.0 copy-start.4
  62.5 1.2 copy-done.4
  63.7 1.2 copy-done.6
  64.9 0.0 collective-permute-start.6
  64.9 4.1 %collective-permute-start.7 = (f32[64,8,128]{2,1,0:T(8,128)S(1)}, f32[64,8,128]{2,1,0:T(8,128)S(1)}, u32[]{:S(2)}, u32[]{:S(2)}) collective-permute-start(f32[64,8,128]{2,1,0:T(8,128)S(1)} %get-tuple-element.50), channel_id=1, source_target_pairs={{16,0},{24,8},{0,16},{8,24},{17,1},{25,9},{1,17},{9,25},{18,2},{26... | collective-permute-start | bytes 786440 | tf_op jit(solution)/shard_map/ppermute | solution.py:531
  69.0 0.0 collective-permute-start.8
  69.0 6.2 %collective-permute-done.6 = f32[64,8,128]{2,1,0:T(8,128)S(1)} collective-permute-done((f32[64,8,128]{2,1,0:T(8,128)S(1)}, f32[64,8,128]{2,1,0:T(8,128)S(1)}, u32[]{:S(2)}, u32[]{:S(2)}) %collective-permute-start.6) | collective-permute-done | bytes 262176 | tf_op jit(solution)/shard_map/ppermute | solution.py:531
  75.2 4.3 %collective-permute-done.7 = f32[64,8,128]{2,1,0:T(8,128)S(1)} collective-permute-done((f32[64,8,128]{2,1,0:T(8,128)S(1)}, f32[64,8,128]{2,1,0:T(8,128)S(1)}, u32[]{:S(2)}, u32[]{:S(2)}) %collective-permute-start.7) | collective-permute-done | bytes 262176 | tf_op jit(solution)/shard_map/ppermute | solution.py:531
  79.6 0.1 collective-permute-done.8
  79.7 2.7 %collective-permute-start.10 = (f32[64,32,128]{2,1,0:T(8,128)S(1)}, f32[64,32,128]{2,1,0:T(8,128)S(1)}, u32[]{:S(2)}, u32[]{:S(2)}) collective-permute-start(f32[64,32,128]{2,1,0:T(8,128)S(1)} %constant_dynamic-update-slice_fusion.own), channel_id=1, source_target_pairs={{32,0},{64,32},{96,64},{128,96},{160,128},{192,160},{224,192},{0,2... | collective-permute-start | bytes 3145736 | tf_op jit(solution)/shard_map/ppermute | solution.py:531
  82.4 0.0 collective-permute-start.9
  82.4 21.5 %collective-permute-done.10.above = f32[64,32,128]{2,1,0:T(8,128)S(1)} collective-permute-done((f32[64,32,128]{2,1,0:T(8,128)S(1)}, f32[64,32,128]{2,1,0:T(8,128)S(1)}, u32[]{:S(2)}, u32[]{:S(2)}) %collective-permute-start.10) | collective-permute-done | bytes 1048608 | tf_op jit(solution)/shard_map/ppermute | solution.py:531
  104.0 3.4 %collective-permute-done.9.below = f32[64,32,128]{2,1,0:T(8,128)S(1)} collective-permute-done((f32[64,32,128]{2,1,0:T(8,128)S(1)}, f32[64,32,128]{2,1,0:T(8,128)S(1)}, u32[]{:S(2)}, u32[]{:S(2)}) %collective-permute-start.9) | collective-permute-done | bytes 1048608 | tf_op jit(solution)/shard_map/ppermute | solution.py:526
  107.4 11.2 %down.2 = (f32[48,32,128]{2,1,0:T(8,128)S(1)}, f32[48,32,128]{2,1,0:T(8,128)S(1)}, f32[48,32,128]{2,1,0:T(8,128)S(1)}, f32[48,32,128]{2,1,0:T(8,128)S(1)}, f32[4...) custom-call(s32[3]{0:T(128)S(1)} %pad_add_fusion.where, ...), custom_call_target="tpu_custom_call" | custom-call | tf_op jit(solution)/shard_map/down/pallas_call | solution.py:512
  118.6 0.0 copy-done
  118.6 0.0 copy-done.2
  118.6 0.0 collective-permute-start.12
  118.6 0.5 collective-permute-start.11
  119.1 1.4 collective-permute-done.12.above
  120.5 3.3 %collective-permute-done.11.below = f32[16,8,128]{2,1,0:T(8,128)S(1)} collective-permute-done((f32[16,8,128]{2,1,0:T(8,128)S(1)}, f32[16,8,128]{2,1,0:T(8,128)S(1)}, u32[]{:S(2)}, u32[]{:S(2)}) %collective-permute-start.11) | collective-permute-done | bytes 65568 | tf_op jit(solution)/shard_map/ppermute | solution.py:526
  123.9 0.1 spread.2
  124.0 21.4 %all_to_all.10.gathered = f32[8,16,8,128]{3,2,1,0:T(8,128)S(1)} all-to-all(f32[8,16,8,128]{3,2,1,0:T(8,128)S(1)} %spread.2), channel_id=1, replica_groups=mesh['gx'=8,'gy'=4,'gz'=8] {'gx'}, dimensions={0} | all-to-all | bytes 1048576 | tf_op jit(solution)/shard_map/all_to_all | solution.py:576
  145.4 23.0 %up.1 = (f32[32,8,128]{2,1,0:T(8,128)S(1)}, f32[32,8,128]{2,1,0:T(8,128)S(1)}, f32[32,8,128]{2,1,0:T(8,128)S(1)}, f32[32,8,128]{2,1,0:T(8,128)S(1)}, f32[32,8,12...) custom-call(s32[3]{0:T(128)S(1)} %pad_add_fusion.where, ...), custom_call_target="tpu_custom_call" | custom-call | tf_op jit(solution)/shard_map/up/pallas_call | solution.py:512
  168.5 0.0 copy-start.5
  168.5 3.8 %collective-permute-start.15 = (f32[16,8,128]{2,1,0:T(8,128)S(1)}, f32[16,8,128]{2,1,0:T(8,128)S(1)}, u32[]{:S(2)}, u32[]{:S(2)}) collective-permute-start(f32[16,8,128]{2,1,0:T(8,128)S(1)} %get-tuple-element.73), channel_id=1, source_target_pairs={{24,0},{0,8},{8,16},{16,24},{25,1},{1,9},{9,17},{17,25},{26,2},{2,... | collective-permute-start | bytes 196616 | tf_op jit(solution)/shard_map/ppermute | solution.py:531
  172.2 0.2 collective-permute-start.14
  172.5 0.7 collective-permute-start.13
  173.2 5.5 %collective-permute-done.13 = f32[16,8,128]{2,1,0:T(8,128)S(1)} collective-permute-done((f32[16,8,128]{2,1,0:T(8,128)S(1)}, f32[16,8,128]{2,1,0:T(8,128)S(1)}, u32[]{:S(2)}, u32[]{:S(2)}) %collective-permute-start.13) | collective-permute-done | bytes 65568 | tf_op jit(solution)/shard_map/ppermute | solution.py:531
  178.7 0.0 collective-permute-done.14
  178.7 0.0 collective-permute-done.15
  178.7 0.0 copy-start.1
  178.7 0.0 copy-start.3
  178.7 0.3 collective-permute-start.17
  179.1 2.0 collective-permute-start.16
  181.1 4.3 %collective-permute-done.17.above = f32[16,32,128]{2,1,0:T(8,128)S(1)} collective-permute-done((f32[16,32,128]{2,1,0:T(8,128)S(1)}, f32[16,32,128]{2,1,0:T(8,128)S(1)}, u32[]{:S(2)}, u32[]{:S(2)}) %collective-permute-start.17) | collective-permute-done | bytes 262176 | tf_op jit(solution)/shard_map/ppermute | solution.py:531
  185.4 1.3 collective-permute-done.16.below
  186.7 6.3 %down.3 = (f32[48,32,128]{2,1,0:T(8,128)S(1)}, f32[48,32,128]{2,1,0:T(8,128)S(1)}, f32[24,16,128]{2,1,0:T(8,128)S(1)}, f32[24,16,128]{2,1,0:T(8,128)S(1)}, f32[4,8,128]{2,1,0:T(8,128)S(1)}) custom-call(s32[3]{0:T(128)S(1)} %pad_add_fusion.where, f32[16,32,128]{2,1,0:T(8,128)S(1)} %constant_dynamic-update-slice_fusion.4.own, ...), custom_call_target="tpu_custom_call" | custom-call | tf_op jit(solution)/shard_map/down/pallas_call | solution.py:512
  193.0 0.0 collective-permute-start.19
  193.0 0.5 collective-permute-start.18
  193.5 0.9 collective-permute-done.19.above
  194.5 3.0 %collective-permute-done.18.below = f32[4,8,128]{2,1,0:T(8,128)S(1)} collective-permute-done((f32[4,8,128]{2,1,0:T(8,128)S(1)}, f32[4,8,128]{2,1,0:T(8,128)S(1)}, u32[]{:S(2)}, u32[]{:S(2)}) %collective-permute-start.18) | collective-permute-done | bytes 16416 | tf_op jit(solution)/shard_map/ppermute | solution.py:526
  197.5 0.1 spread.3
  197.6 12.9 %all_to_all.11.gathered = f32[8,4,8,128]{3,2,1,0:T(8,128)S(1)} all-to-all(f32[8,4,8,128]{3,2,1,0:T(8,128)S(1)} %spread.3), channel_id=1, replica_groups=mesh['gx'=8,'gy'=4,'gz'=8] {'gx'}, dimensions={0} | all-to-all | bytes 262144 | tf_op jit(solution)/shard_map/all_to_all | solution.py:576
  210.6 16.3 %up_last.1 = (f32[32,16,128]{2,1,0:T(8,128)}, f32[32,16,128]{2,1,0:T(8,128)}) custom-call(s32[3]{0:T(128)S(1)} %pad_add_fusion.where, f32[8,4,8,128]{3,2,1,0:T(8,128)S(1)} %all_to_all.11.gathered, f32[32,8,128]{2,1,0:T(8,128)S(1)} %get-tuple-element.75.refs_0_, f32[32,8,128]{2,1,0:T(8,128)S(1)} %get-tuple-element.76.refs_1_, ...), custom_call_target="tpu_custom_call" | custom-call | tf_op jit(solution)/shard_map/up_last/pallas_call | solution.py:512
  (15 shorter events, 0.1 us)
Async XLA Ops:
  0.6 1.0 copy-start.7
  1.6 0.9 copy-start.8
  2.7 7.0 %collective-permute-start = (f32[32,16,128]{2,1,0:T(8,128)S(1)}, f32[32,16,128]{2,1,0:T(8,128)S(1)}, u32[]{:S(2)}, u32[]{:S(2)}) collective-permute-start(f32[32,16,128]{2,1,0:T(8,128)S(1)} %get-tuple-element.44), channel_id=1, source_target_pairs={{0,1},{1,2},{2,3},{3,4},{4,5},{5,6},{6,7},{7,0},{8,9},{9,10},{10,1... | collective-permute-start | bytes 786440 | tf_op jit(solution)/shard_map/ppermute | solution.py:526
  2.7 7.0 %collective-permute-start.1 = (f32[32,16,128]{2,1,0:T(8,128)S(1)}, f32[32,16,128]{2,1,0:T(8,128)S(1)}, u32[]{:S(2)}, u32[]{:S(2)}) collective-permute-start(f32[32,16,128]{2,1,0:T(8,128)S(1)} %get-tuple-element.45), channel_id=1, source_target_pairs={{1,0},{2,1},{3,2},{4,3},{5,4},{6,5},{7,6},{0,7},{9,8},{10,9},{11,1... | collective-permute-start | bytes 786440 | tf_op jit(solution)/shard_map/ppermute | solution.py:531
  9.9 16.3 %collective-permute-start.3 = (f32[68,8,256]{2,1,0:T(8,128)S(1)}, f32[68,8,256]{2,1,0:T(8,128)S(1)}, u32[]{:S(2)}, u32[]{:S(2)}) collective-permute-start(f32[68,8,256]{2,1,0:T(8,128)S(1)} %get-tuple-element.46.lower), channel_id=1, source_target_pairs={{8,0},{16,8},{24,16},{0,24},{9,1},{17,9},{25,17},{1,25},{10,2},{18... | collective-permute-start | bytes 1671176 | tf_op jit(solution)/shard_map/ppermute | solution.py:531
  10.8 15.4 %collective-permute-start.2 = (f32[68,8,256]{2,1,0:T(8,128)S(1)}, f32[68,8,256]{2,1,0:T(8,128)S(1)}, u32[]{:S(2)}, u32[]{:S(2)}) collective-permute-start(f32[68,8,256]{2,1,0:T(8,128)S(1)} %get-tuple-element.47.upper), channel_id=1, source_target_pairs={{0,8},{8,16},{16,24},{24,0},{1,9},{9,17},{17,25},{25,1},{2,10},{10... | collective-permute-start | bytes 1671176 | tf_op jit(solution)/shard_map/ppermute | solution.py:526
  27.3 19.2 %collective-permute-start.4 = (f32[18,32,256]{2,1,0:T(8,128)}, f32[18,32,256]{2,1,0:T(8,128)S(1)}, u32[]{:S(2)}, u32[]{:S(2)}) collective-permute-start(f32[18,32,256]{2,1,0:T(8,128)} %get-tuple-element.48), channel_id=1, source_target_pairs={{0,32},{32,64},{64,96},{96,128},{128,160},{160,192},{192,224},{224... | collective-permute-start | bytes 1769480 | tf_op jit(solution)/shard_map/ppermute | solution.py:526
  29.2 17.3 %collective-permute-start.5 = (f32[18,32,256]{2,1,0:T(8,128)}, f32[18,32,256]{2,1,0:T(8,128)S(1)}, u32[]{:S(2)}, u32[]{:S(2)}) collective-permute-start(f32[18,32,256]{2,1,0:T(8,128)} %get-tuple-element.49), channel_id=1, source_target_pairs={{32,0},{64,32},{96,64},{128,96},{160,128},{192,160},{224,192},{0,2... | collective-permute-start | bytes 1769480 | tf_op jit(solution)/shard_map/ppermute | solution.py:531
  62.5 1.2 copy-start.4
  63.7 1.2 copy-start.6
  64.9 53.7 %copy-start = (f32[48,32,256]{2,1,0:T(8,128)}, f32[48,32,256]{2,1,0:T(8,128)S(1)}, u32[]{:S(2)}) copy-start(f32[48,32,256]{2,1,0:T(8,128)S(1)} %get-tuple-element.68.refs_16_.refs_21_) | copy-start | bytes 4718596
  64.9 53.7 %copy-start.2 = (f32[48,32,256]{2,1,0:T(8,128)}, f32[48,32,256]{2,1,0:T(8,128)S(1)}, u32[]{:S(2)}) copy-start(f32[48,32,256]{2,1,0:T(8,128)S(1)} %get-tuple-element.69.refs_17_.refs_22_) | copy-start | bytes 4718596
  64.9 10.3 %collective-permute-start.6 = (f32[64,8,128]{2,1,0:T(8,128)S(1)}, f32[64,8,128]{2,1,0:T(8,128)S(1)}, u32[]{:S(2)}, u32[]{:S(2)}) collective-permute-start(f32[64,8,128]{2,1,0:T(8,128)S(1)} %get-tuple-element.50), channel_id=1, source_target_pairs={{8,0},{16,8},{24,16},{0,24},{9,1},{17,9},{25,17},{1,25},{10,2},{18... | collective-permute-start | bytes 786440 | tf_op jit(solution)/shard_map/ppermute | solution.py:531
  64.9 14.7 %collective-permute-start.7 = (f32[64,8,128]{2,1,0:T(8,128)S(1)}, f32[64,8,128]{2,1,0:T(8,128)S(1)}, u32[]{:S(2)}, u32[]{:S(2)}) collective-permute-start(f32[64,8,128]{2,1,0:T(8,128)S(1)} %get-tuple-element.50), channel_id=1, source_target_pairs={{16,0},{24,8},{0,16},{8,24},{17,1},{25,9},{1,17},{9,25},{18,2},{26... | collective-permute-start | bytes 786440 | tf_op jit(solution)/shard_map/ppermute | solution.py:531
  69.0 10.7 %collective-permute-start.8 = (f32[64,8,128]{2,1,0:T(8,128)S(1)}, f32[64,8,128]{2,1,0:T(8,128)S(1)}, u32[]{:S(2)}, u32[]{:S(2)}) collective-permute-start(f32[64,8,128]{2,1,0:T(8,128)S(1)} %get-tuple-element.50), channel_id=1, source_target_pairs={{24,0},{0,8},{8,16},{16,24},{25,1},{1,9},{9,17},{17,25},{26,2},{2,... | collective-permute-start | bytes 786440 | tf_op jit(solution)/shard_map/ppermute | solution.py:531
  79.7 24.2 %collective-permute-start.10 = (f32[64,32,128]{2,1,0:T(8,128)S(1)}, f32[64,32,128]{2,1,0:T(8,128)S(1)}, u32[]{:S(2)}, u32[]{:S(2)}) collective-permute-start(f32[64,32,128]{2,1,0:T(8,128)S(1)} %constant_dynamic-update-slice_fusion.own), channel_id=1, source_target_pairs={{32,0},{64,32},{96,64},{128,96},{160,128},{192,160},{224,192},{0,2... | collective-permute-start | bytes 3145736 | tf_op jit(solution)/shard_map/ppermute | solution.py:531
  82.4 25.0 %collective-permute-start.9 = (f32[64,32,128]{2,1,0:T(8,128)S(1)}, f32[64,32,128]{2,1,0:T(8,128)S(1)}, u32[]{:S(2)}, u32[]{:S(2)}) collective-permute-start(f32[64,32,128]{2,1,0:T(8,128)S(1)} %constant_dynamic-update-slice_fusion.own), channel_id=1, source_target_pairs={{0,32},{32,64},{64,96},{96,128},{128,160},{160,192},{192,224},{224... | collective-permute-start | bytes 3145736 | tf_op jit(solution)/shard_map/ppermute | solution.py:526
  118.6 1.9 collective-permute-start.12
  118.6 5.2 %collective-permute-start.11 = (f32[16,8,128]{2,1,0:T(8,128)S(1)}, f32[16,8,128]{2,1,0:T(8,128)S(1)}, u32[]{:S(2)}, u32[]{:S(2)}) collective-permute-start(f32[16,8,128]{2,1,0:T(8,128)S(1)} %get-tuple-element.51.own), channel_id=1, source_target_pairs={{0,1},{1,2},{2,3},{3,4},{4,5},{5,6},{6,7},{7,0},{8,9},{9,10},{10,1... | collective-permute-start | bytes 196616 | tf_op jit(solution)/shard_map/ppermute | solution.py:526
  168.5 24.6 %copy-start.5 = (f32[48,32,256]{2,1,0:T(8,128)}, f32[48,32,256]{2,1,0:T(8,128)S(1)}, u32[]{:S(2)}) copy-start(f32[48,32,256]{2,1,0:T(8,128)S(1)} %get-tuple-element.84.refs_24_) | copy-start | bytes 4718596
  168.5 10.2 %collective-permute-start.15 = (f32[16,8,128]{2,1,0:T(8,128)S(1)}, f32[16,8,128]{2,1,0:T(8,128)S(1)}, u32[]{:S(2)}, u32[]{:S(2)}) collective-permute-start(f32[16,8,128]{2,1,0:T(8,128)S(1)} %get-tuple-element.73), channel_id=1, source_target_pairs={{24,0},{0,8},{8,16},{16,24},{25,1},{1,9},{9,17},{17,25},{26,2},{2,... | collective-permute-start | bytes 196616 | tf_op jit(solution)/shard_map/ppermute | solution.py:531
  172.2 6.4 %collective-permute-start.14 = (f32[16,8,128]{2,1,0:T(8,128)S(1)}, f32[16,8,128]{2,1,0:T(8,128)S(1)}, u32[]{:S(2)}, u32[]{:S(2)}) collective-permute-start(f32[16,8,128]{2,1,0:T(8,128)S(1)} %get-tuple-element.73), channel_id=1, source_target_pairs={{16,0},{24,8},{0,16},{8,24},{17,1},{25,9},{1,17},{9,25},{18,2},{26... | collective-permute-start | bytes 196616 | tf_op jit(solution)/shard_map/ppermute | solution.py:531
  172.5 6.2 %collective-permute-start.13 = (f32[16,8,128]{2,1,0:T(8,128)S(1)}, f32[16,8,128]{2,1,0:T(8,128)S(1)}, u32[]{:S(2)}, u32[]{:S(2)}) collective-permute-start(f32[16,8,128]{2,1,0:T(8,128)S(1)} %get-tuple-element.73), channel_id=1, source_target_pairs={{8,0},{16,8},{24,16},{0,24},{9,1},{17,9},{25,17},{1,25},{10,2},{18... | collective-permute-start | bytes 196616 | tf_op jit(solution)/shard_map/ppermute | solution.py:531
  178.7 31.8 %copy-start.1 = (f32[48,32,256]{2,1,0:T(8,128)S(1)}, f32[48,32,256]{2,1,0:T(8,128)}, u32[]{:S(2)}) copy-start(f32[48,32,256]{2,1,0:T(8,128)} %copy-done) | copy-start | bytes 4718596
  178.7 31.8 %copy-start.3 = (f32[48,32,256]{2,1,0:T(8,128)S(1)}, f32[48,32,256]{2,1,0:T(8,128)}, u32[]{:S(2)}) copy-start(f32[48,32,256]{2,1,0:T(8,128)} %copy-done.2) | copy-start | bytes 4718596
  178.7 6.7 %collective-permute-start.17 = (f32[16,32,128]{2,1,0:T(8,128)S(1)}, f32[16,32,128]{2,1,0:T(8,128)S(1)}, u32[]{:S(2)}, u32[]{:S(2)}) collective-permute-start(f32[16,32,128]{2,1,0:T(8,128)S(1)} %constant_dynamic-update-slice_fusion.4.own), channel_id=1, source_target_pairs={{32,0},{64,32},{96,64},{128,96},{160,128},{192,160},{224,192},{0,2... | collective-permute-start | bytes 786440 | tf_op jit(solution)/shard_map/ppermute | solution.py:531
  179.1 7.7 %collective-permute-start.16 = (f32[16,32,128]{2,1,0:T(8,128)S(1)}, f32[16,32,128]{2,1,0:T(8,128)S(1)}, u32[]{:S(2)}, u32[]{:S(2)}) collective-permute-start(f32[16,32,128]{2,1,0:T(8,128)S(1)} %constant_dynamic-update-slice_fusion.4.own), channel_id=1, source_target_pairs={{0,32},{32,64},{64,96},{96,128},{128,160},{160,192},{192,224},{224... | collective-permute-start | bytes 786440 | tf_op jit(solution)/shard_map/ppermute | solution.py:526
  193.0 1.5 collective-permute-start.19
  193.0 4.5 %collective-permute-start.18 = (f32[4,8,128]{2,1,0:T(8,128)S(1)}, f32[4,8,128]{2,1,0:T(8,128)S(1)}, u32[]{:S(2)}, u32[]{:S(2)}) collective-permute-start(f32[4,8,128]{2,1,0:T(8,128)S(1)} %get-tuple-element.74.own), channel_id=1, source_target_pairs={{0,1},{1,2},{2,3},{3,4},{4,5},{5,6},{6,7},{7,0},{8,9},{9,10},{10,1... | collective-permute-start | bytes 49160 | tf_op jit(solution)/shard_map/ppermute | solution.py:526
where the time goes:
time: 227 us
  waiting for transfers between devices  85.7 us (38%)
  Pallas kernels  74.5 us (33%)
  blocking collectives  34.4 us (15%)
  starting transfers between devices  27 us (12%)
  local copies, waits for them, and re-layouts  4.4 us (2%)
    pallas_call x10, Pallas kernels, call(): pl.pallas_call(kernel, out_shape=[jax.ShapeDtypeStruct(s, F32) for s in o...  74.5 us
    ppermute x13, waiting for transfers between devices, from_above(): return lax.ppermute(array, axis, [((i + by) % n, i) for i in range(n)])  57.3 us
    all_to_all x2, blocking collectives, body(): gathered = lax.all_to_all(copies, 'gx', 0, 0)  34.4 us
    ppermute x7, waiting for transfers between devices, from_below(): return lax.ppermute(array, axis, [(i, (i + 1) % n) for i in range(n)])  28.5 us
    ppermute x13, starting transfers between devices, from_above(): return lax.ppermute(array, axis, [((i + by) % n, i) for i in range(n)])  19.6 us
    ppermute x7, starting transfers between devices, from_below(): return lax.ppermute(array, axis, [(i, (i + 1) % n) for i in range(n)])  7.37 us
  transfers between devices with their start and end apart: 20, of which 15 were waited for; matrix products, arithmetic and copies ran while one was open for 0% of the time, Pallas kernels for 0%

commit v1 on v0

--- a/solution.py
+++ b/solution.py
@@ -23,6 +23,9 @@
 X1, Y1G, Z1 = 48, 8, 128
 X2 = 24
 F32 = jnp.float32
+BF16 = jnp.bfloat16
+DOWN, UP = 3, 3
+UC, B0, U0, B1 = 4, 4, 2, 16
 
 
 def chebyshev(low, degree):
@@ -50,8 +53,22 @@
     return lax.broadcasted_iota(jnp.int32, shape, dim)
 
 
-def dot(left, right):
-    return jnp.dot(left, right, precision=lax.Precision.HIGHEST, preferred_element_type=F32)
+def split(values, terms):
+    parts = []
+    for n in range(terms):
+        part = values.astype(BF16)
+        parts.append(part)
+        if n + 1 < terms:
+            values = values - part.astype(F32)
+    return parts
+
+
+def times(values, matrix, terms):
+    return sum(jnp.dot(p, matrix, preferred_element_type=F32) for p in split(values, terms))
+
+
+def times_left(matrix, values, terms):
+    return sum(jnp.dot(matrix, p, preferred_element_type=F32) for p in split(values, terms))
 
 
 def lane_pairs(fine, weight, odd_only=False):
@@ -62,7 +79,7 @@
     hit = half == iota((fine, 128), 1)
     if odd_only:
         hit = hit & ((z & 1) == 1)
-    return jnp.where(hit, weight, 0.0).astype(F32)
+    return jnp.where(hit, weight, 0.0).astype(BF16)
 
 
 def lane_copies(fine):
@@ -70,7 +87,7 @@
     half = z >> 1
     if fine == 128:
         half = jnp.where(z >= 96, half + 64, half)
-    return jnp.where(half == iota((128, fine), 0), 1.0, 0.0).astype(F32)
+    return jnp.where(half == iota((128, fine), 0), 1.0, 0.0).astype(BF16)
 
 
 def row_pairs(rows, odd_x=False, odd_y=False):
@@ -84,7 +101,7 @@
         hit = hit & ((x & 1) == 1)
     if odd_y:
         hit = hit & ((y & 1) == 1)
-    return jnp.where(hit, 1.0, 0.0).astype(F32)
+    return jnp.where(hit, 1.0, 0.0).astype(BF16)
 
 
 def row_copies(rows):
@@ -92,18 +109,18 @@
     shift = rows.bit_length() - 1
     f, c = iota(shape, 0), iota(shape, 1)
     hit = ((f >> (shift + 1)) == (c >> (shift - 1))) & (((f & (rows - 1)) >> 1) == (c & (rows // 2 - 1)))
-    return jnp.where(hit, 1.0, 0.0).astype(F32)
+    return jnp.where(hit, 1.0, 0.0).astype(BF16)
 
 
 def coarsen(block, rows_matrix, lanes_matrix):
     planes, rows, lanes = block.shape
-    out = dot(dot(rows_matrix, block.reshape(planes * rows, lanes)), lanes_matrix)
+    out = times(times_left(rows_matrix, block.reshape(planes * rows, lanes), DOWN), lanes_matrix, DOWN)
     return out.reshape(4, rows // 2, 128)
 
 
 def refine(block, rows_matrix, lanes_matrix):
     planes, rows, lanes = block.shape
-    out = dot(rows_matrix, dot(block.reshape(planes * rows, lanes), lanes_matrix))
+    out = times_left(rows_matrix, times(block.reshape(planes * rows, lanes), lanes_matrix, UP), UP)
     return out.reshape(8, 2 * rows, lanes_matrix.shape[1])
 
 
@@ -145,40 +162,27 @@
     return fx, fy, fz, diag, inverse(diag)
 
 
-def loop(start, stop, block, body):
+def loop(start, stop, block, body, unroll=1):
     count = (stop - start) // block
-    assert count * block == stop - start
 
     def step(i, carry):
-        body(start + i * block)
+        body(start + i * block, block)
         return carry
 
-    lax.fori_loop(0, count, step, 0)
-
-
-def send_z(r, mask, to_upper, to_lower):
+    if count:
+        lax.fori_loop(0, count, step, 0, unroll=unroll)
+    rest = stop - start - count * block
+    if rest:
+        body(stop - rest, rest)
+
+
+def send_y(r, mask, to_upper, to_lower):
     density = GAS + (LIQUID - GAS) * mask[...].astype(F32)
-    turned = roll(density, 64, 2)
-    lane = iota(density.shape, 2)
-    to_upper[...] = jnp.where(lane >= 64, r[...], turned)
-    to_lower[...] = jnp.where(lane < 64, r[...], turned)
-
-
-def send_y(r, mask, below, above, to_upper, to_lower):
-    density = GAS + (LIQUID - GAS) * mask[...].astype(F32)
-    low, high = below[...], above[...]
-    lane = iota(density.shape, 2)
-    r_side = jnp.where(lane < 64, high, low)
-    d_side = roll(jnp.where(lane >= 64, high, low), 64, 2)
     for out, rows, line in ((to_upper, slice(8, 16), 7), (to_lower, slice(0, 8), 8)):
-        out[0:BX, :, 0:128] = r[:, rows, :]
-        out[0:BX, :, 128:256] = r_side[:, rows]
-        out[BX : 2 * BX, :, 0:128] = density[:, rows]
-        out[BX : 2 * BX, :, 128:256] = d_side[:, rows]
+        out[0:BX] = r[:, rows, :]
+        out[BX : 2 * BX] = density[:, rows]
         for x in range(BX):
-            at = 2 * BX + x // 8
-            out[at, x % 8 : x % 8 + 1, 0:128] = density[x, line : line + 1]
-            out[at, x % 8 : x % 8 + 1, 128:256] = d_side[x, line : line + 1]
+            out[2 * BX + x // 8, x % 8 : x % 8 + 1] = density[x, line : line + 1]
 
 
 def send_x(lower, upper, below, above, to_upper, to_lower):
@@ -189,30 +193,49 @@
             out[8:17, rows] = source[BX + d_at : BX + d_at + 9]
         out[17, 0:8] = below[2 * BX + pack]
         out[17, 8:16] = above[2 * BX + pack]
-        out[17, 16:32] = jnp.zeros((16, Z0), F32)
+        out[17, 16:32] = jnp.zeros((16, 128), F32)
+
+
+def send_z(lower, upper, below, above, x_below, x_above, to_upper, to_lower):
+    for out, high in ((to_upper, True), (to_lower, False)):
+        def beside(one, two):
+            lane = iota(one.shape, one.ndim - 1)
+            return jnp.where((lane >= 64) == high, one, roll(two, 64, one.ndim - 1))
+
+        out[0:8] = beside(x_below[0:8], x_below[9:17])
+        out[40:48] = beside(x_above[0:8], x_above[8:16])
+        out[48] = beside(x_below[8], x_above[16])
+        for tile, source in enumerate((lower, upper, above, below)):
+            out[8:40, 8 * tile : 8 * tile + 8] = beside(source[0:BX], source[BX : 2 * BX])
+        out[49, 0:8] = beside(x_below[17, 0:8], x_below[17, 8:16])
+        for n in range(4):
+            at = 8 * (n + 1)
+            out[49 + at // 32, at % 32 : at % 32 + 8] = beside(below[2 * BX + n], above[2 * BX + n])
+        out[50, 8:16] = beside(x_above[17, 0:8], x_above[17, 8:16])
+        out[50, 16:32] = jnp.zeros((16, 128), F32)
 
 
 def presmooth_0(where, r, faces, inv, d0, d1, start, stop, have_first):
     if not have_first:
-        def first(at):
-            here = pl.ds(at, 2)
+        def first(at, n):
+            here = pl.ds(at, n)
             d0[here] = (FIRST * r[here]) * inv[here]
 
-        loop(start, stop, 2, first)
-
-    def second(at):
-        here = pl.ds(at, 2)
-        left = r[here] - apply_at(d0, at, 2, faces)
+        loop(start, stop, B0, first, U0)
+
+    def second(at, n):
+        here = pl.ds(at, n)
+        left = r[here] - apply_at(d0, at, n, faces)
         r[here] = left
         d1[here] = KEEP * d0[here] + GAIN * (left * inv[here])
 
-    loop(start + 1, stop - 1, 2, second)
-
-    def third(at):
-        here = pl.ds(at, 2)
-        r[here] = r[here] - apply_at(d1, at, 2, faces)
-
-    loop(start + 2, stop - 2, 2, third)
+    loop(start + 1, stop - 1, B0, second, U0)
+
+    def third(at, n):
+        here = pl.ds(at, n)
+        r[here] = r[here] - apply_at(d1, at, n, faces)
+
+    loop(start + 2, stop - 2, B0, third, U0)
 
 
 def restrict_0(r, out):
@@ -230,39 +253,60 @@
     total[...] = value
 
 
-def begin(sizes, where, lower, upper, below, above, x_below, x_above,
+def face(total):
+    return jnp.where(total < 5.0, 1.0, jnp.where(total < 15.0, 2.0 / 11.0, 0.1))
+
+
+def begin(sizes, where, lower, upper, below, above, x_below, x_above, z_below, z_above,
           fx, fy, fz, diag, inv, r, total, packed, rho, low, up, raw_x, raw_y, raw_z, d0, d1):
     nx, ny, nz = sizes
     gx0, gy0, gz0 = where[0] * BX, where[1] * BY, where[2] * BZ
-    r[0:8] = x_below[0:8]
-    r[40:48] = x_above[0:8]
-    rho[0:9] = x_below[8:17]
-    rho[41:50] = x_above[8:17]
+    own, side = slice(0, 128), slice(128, 256)
+    r[0:8, :, own] = x_below[0:8]
+    r[40:48, :, own] = x_above[0:8]
+    rho[0:9, :, own] = x_below[8:17]
+    rho[41:50, :, own] = x_above[8:17]
     for tile, source in enumerate((lower, upper, above, below)):
         rows = slice(8 * tile, 8 * tile + 8)
-        r[8:40, rows] = source[0:BX]
-        rho[9:41, rows] = source[BX : 2 * BX]
-    low[0:8] = x_below[17, 0:8]
-    up[0:8] = x_below[17, 8:16]
-    low[40:48] = x_above[17, 0:8]
-    up[40:48] = x_above[17, 8:16]
-    low[8:40] = below[2 * BX : 2 * BX + 4].reshape(BX, Z0)
-    up[8:40] = above[2 * BX : 2 * BX + 4].reshape(BX, Z0)
-
-    def plane(p):
+        r[8:40, rows, own] = source[0:BX]
+        rho[9:41, rows, own] = source[BX : 2 * BX]
+    low[0:8, own] = x_below[17, 0:8]
+    up[0:8, own] = x_below[17, 8:16]
+    low[40:48, own] = x_above[17, 0:8]
+    up[40:48, own] = x_above[17, 8:16]
+    for n in range(4):
+        low[8 + 8 * n : 16 + 8 * n, own] = below[2 * BX + n]
+        up[8 + 8 * n : 16 + 8 * n, own] = above[2 * BX + n]
+
+    def sides(at):
+        one, two = z_above[at], z_below[at]
+        axis = one.ndim - 1
+        lane = iota(one.shape, axis)
+        return jnp.where(lane < 64, one, two), roll(jnp.where(lane >= 64, one, two), 64, axis)
+
+    def side_planes(p, n):
+        r[pl.ds(p, n), :, side], rho[pl.ds(p + 1, n), :, side] = sides(pl.ds(p, n))
+
+    loop(0, X0, 4, side_planes)
+    rho[0, :, side], rho[49, :, side] = sides(48)
+    low[0:32, side], up[0:32, side] = sides(49)
+    low_rest, up_rest = sides(50)
+    low[32:48, side], up[32:48, side] = low_rest[0:16], up_rest[0:16]
+
+    def plane(p, n):
         shape = (Y0, Z0)
         row, lane = iota(shape, 0), iota(shape, 1)
         gy = gy0 + jnp.where(row < 24, row, row - 32)
         gz = gz0 + jnp.where(lane < 192, lane, lane - 256)
         gx = gx0 + p - WX
         c = rho[p + 1]
-        f_x = 2.0 / (c + jnp.where(gx == nx - 1, GAS, rho[p + 2]))
-        l_x = jnp.where(gx == 0, 0.0, 2.0 / (c + rho[p]))
+        f_x = face(c + jnp.where(gx == nx - 1, GAS, rho[p + 2]))
+        l_x = jnp.where(gx == 0, 0.0, face(c + rho[p]))
         over = jnp.where(row == 23, up[pl.ds(p, 1)], roll(c, -1, 0))
         under = jnp.where(row == 24, low[pl.ds(p, 1)], roll(c, 1, 0))
-        f_y = 2.0 / (c + jnp.where(gy == ny - 1, GAS, over))
-        l_y = jnp.where(gy == 0, 0.0, 2.0 / (c + under))
-        f_z = 2.0 / (c + jnp.where(gz == nz - 1, GAS, roll(c, -1, 1)))
+        f_y = face(c + jnp.where(gy == ny - 1, GAS, over))
+        l_y = jnp.where(gy == 0, 0.0, face(c + under))
+        f_z = face(c + jnp.where(gz == nz - 1, GAS, roll(c, -1, 1)))
         l_z = jnp.where(gz == 0, 0.0, roll(f_z, 1, 1))
         d = f_x + l_x + f_y + l_y + f_z + l_z
         i = 1.0 / d
@@ -276,7 +320,7 @@
         fy[p] = jnp.where((gy == ny - 1) | (gy == -1), 0.0, f_y)
         fz[p] = jnp.where((gz == nz - 1) | (gz == -1), 0.0, f_z)
 
-    loop(0, X0, 1, plane)
+    loop(0, X0, 1, plane, UC)
     faces = (fx, fy, fz, diag)
     presmooth_0(where, r, faces, inv, d0, d1, 0, X0, True)
     add_own(total, (d0, d1), True)
@@ -299,13 +343,13 @@
 
 
 def relax_1(r, faces, inv, d0, d1, start, stop):
-    def second(at):
-        here = pl.ds(at, 2)
-        left = r[here] - apply_at(d0, at, 2, faces)
+    def second(at, n):
+        here = pl.ds(at, n)
+        left = r[here] - apply_at(d0, at, n, faces)
         r[here] = left
         d1[here] = KEEP * d0[here] + GAIN * (left * inv[here])
 
-    loop(start, stop, 2, second)
+    loop(start, stop, B1, second)
 
 
 def down(sizes, first, where, own, below, above, *refs):
@@ -332,21 +376,22 @@
         ):
             coarse.append(jnp.concatenate(
                 [coarsen(raw[8 * g : 8 * g + 8], rows_matrix, columns) for g in range(6)], 0))
-        shape = (2, ny1, 128)
+        shape = (B1, ny1, 128)
         gy = lax.rem(where[1] * 8 + iota(shape, 1), n1[1])
         lane = iota(shape, 2)
         gz = where[2] * 64 + jnp.where(lane < 96, lane, lane - 128)
 
-        def planes(n):
-            at = X1 - 2 - n
-            here = pl.ds(at, 2)
+        def planes(n, count):
+            at = X1 - B1 - n
+            here = pl.ds(at, B1)
             gx = where[0] * 16 + at - 16 + iota(shape, 0)
-            before = jnp.concatenate([fx[pl.ds(jnp.maximum(at - 1, 0), 1)], fx[pl.ds(at, 1)]], 0)
-            level = level_of(fx[here], before, fy[here], fz[here], gx, gy, gz, n1)
+            c = fx[here]
+            before = jnp.concatenate([fx[pl.ds(jnp.maximum(at - 1, 0), 1)], c[:-1]], 0)
+            level = level_of(c, before, fy[here], fz[here], gx, gy, gz, n1)
             fx[here], fy[here], fz[here], diag[here], inv[here] = level
             d0[here] = (FIRST * r[here]) * level[4]
 
-        loop(0, X1, 2, planes)
+        loop(0, X1, B1, planes)
         shape = (X2, ny2, 128)
         lane = iota(shape, 2)
         at_2 = (
@@ -362,23 +407,23 @@
             (row_pairs(ny2, odd_y=True), lanes),
             (row_pairs(ny2), odd_lanes),
         )):
-            packed[4 * (n + 1) : 4 * (n + 2)] = coarsen(raw_2[n][8:16], rows_matrix, columns)
+            coarse[n] = coarsen(raw_2[n][8:16], rows_matrix, columns)
     else:
-        def begin_1(at):
-            here = pl.ds(at, 2)
+        def begin_1(at, n):
+            here = pl.ds(at, n)
             d0[here] = (FIRST * r[here]) * inv[here]
 
-        loop(0, X1, 2, begin_1)
+        loop(0, X1, B1, begin_1)
 
     faces = (fx, fy, fz, diag)
     relax_1(r, faces, inv, d0, d1, 1, X1 - 1)
 
-    def third(at):
-        here = pl.ds(at, 2)
-        r[here] = r[here] - apply_at(d1, at, 2, faces)
+    def third(at, n):
+        here = pl.ds(at, n)
+        r[here] = r[here] - apply_at(d1, at, n, faces)
         e[here] = d0[here] + d1[here]
 
-    loop(2, X1 - 2, 2, third)
+    loop(2, X1 - 2, B1, third)
     e[0:2] = d0[0:2]
     e[X1 - 2 : X1] = d0[X1 - 2 : X1]
     r2 = jnp.concatenate([coarsen(r[8 * g : 8 * g + 8], rows, lanes) for g in range(6)], 0)
@@ -389,16 +434,41 @@
     r2 = r2 - apply_to(d_next, faces_2)
     r2_out[...] = r2
     e2_out[...] = d + d_next
-    packed[0:4] = coarsen(r2[8:16], row_pairs(ny2), lanes)
+    sent = coarsen(r2[8:16], row_pairs(ny2), lanes)
+    if first:
+        lane = iota(sent.shape, 2)
+        for n in range(3):
+            at = 16 * (n + 1)
+            sent = jnp.where(lane < at, sent, roll(coarse[n], at, 2))
+    packed[...] = sent
 
 
 def spread(own, below, above, out):
-    lane = iota(own.shape, 2)
-    values = jnp.where(lane < 16, own[...], 0.0)
-    values = jnp.where((lane >= 16) & (lane < 32), roll(above[...], 16, 2), values)
-    values = jnp.where(lane >= 112, roll(below[...], 112, 2), values)
+    shape = own.shape
+    lane = iota(shape, 2)
+    arrays = 2 * (out.shape[1] // shape[0]) if out.shape[1] > shape[0] else 1
+    values = []
+    for n in range(arrays):
+        start = 64 * (n % 2)
+        here = lane - start
+        value = jnp.where(here < 16, roll(own[...], start - 16 * n, 2), 0.0)
+        value = jnp.where((here >= 16) & (here < 32), roll(above[...], start + 16 - 16 * n, 2), value)
+        value = jnp.where(here >= 48, roll(below[...], start + 48 - 16 * n, 2), value)
+        if n % 2:
+            values[-1] = jnp.where(here < 0, values[-1], value)
+        else:
+            values.append(value)
     for d in range(out.shape[0]):
-        out[d] = values
+        for n, value in enumerate(values):
+            out[d, shape[0] * n : shape[0] * (n + 1)] = value
+
+
+def unspread(gathered, n):
+    count, _, rows, lanes = gathered.shape
+    value = gathered[:, 4 * (n // 2) : 4 * (n // 2) + 4].reshape(4 * count, rows, lanes)
+    lane = iota(value.shape, 2)
+    near, far = (roll(value, 64, 2), value) if n % 2 else (value, roll(value, 64, 2))
+    return jnp.where(lane < 32, near, jnp.where(lane >= 112, far, 0.0))
 
 
 def up(sizes, last, where, gathered, *refs):
@@ -422,9 +492,9 @@
     count = gathered.shape[0]
     ny3 = gathered.shape[2]
     shape = (4 * count, ny3, 128)
-    r3 = gathered[:, 0:4].reshape(shape)
+    r3 = unspread(gathered, 0)
     if first:
-        raw = [gathered[:, 4 * n : 4 * n + 4].reshape(shape) for n in (1, 2, 3)]
+        raw = [unspread(gathered, n) for n in (1, 2, 3)]
         lane = iota(shape, 2)
         at = (
             iota(shape, 0),
@@ -462,23 +532,23 @@
         p1[8 + 8 * g : 16 + 8 * g] = refine(e2[4 + 4 * g : 8 + 4 * g], copies_rows, copies_lanes)
     faces = (fx1, fy1, fz1, diag1)
 
-    def lift_1(at):
-        here = pl.ds(at, 2)
-        left = r1_in[here] - apply_at(p1, at, 2, faces)
+    def lift_1(at, n):
+        here = pl.ds(at, n)
+        left = r1_in[here] - apply_at(p1, at, n, faces)
         r1[here] = left
         a1[here] = (FIRST * left) * inv1[here]
 
-    loop(11, 37, 2, lift_1)
+    loop(11, 37, B1, lift_1)
     relax_1(r1, faces, inv1, a1, b1, 12, 36)
 
-    def sum_1(at):
-        here = pl.ds(at, 4)
+    def sum_1(at, n):
+        here = pl.ds(at, n)
         value = e1_in[here] + p1[here] + a1[here] + b1[here]
         c1[here, 0:8] = value[:, 0:8]
-        tile = (4, 8, 128)
+        tile = (n, 8, 128)
         c1[here, 8:16] = jnp.where(iota(tile, 1) < 4, value[:, 8:16], value[:, -8:])
 
-    loop(12, 36, 4, sum_1)
+    loop(12, 36, B1, sum_1)
 
     copies_rows, copies_lanes = row_copies(32), lane_copies(256)
     for g in range(6):
@@ -486,13 +556,13 @@
     faces = (fx, fy, fz, diag)
     begin_at, end_at = (6, 42) if last else (2, 46)
 
-    def lift_0(at):
-        here = pl.ds(at, 2)
-        left = r_in[here] - apply_at(p0, at, 2, faces)
+    def lift_0(at, n):
+        here = pl.ds(at, n)
+        left = r_in[here] - apply_at(p0, at, n, faces)
         r[here] = left
         d0[here] = (FIRST * left) * inv[here]
 
-    loop(begin_at, end_at, 2, lift_0)
+    loop(begin_at, end_at, B0, lift_0, U0)
     presmooth_0(where, r, faces, inv, d0, d1, begin_at, end_at, True)
     if last:
         pressure[...] = total_in[...]
@@ -536,18 +606,18 @@
     sizes = (nx * BX, ny * BY, nz * BZ)
     where = jnp.stack([lax.axis_index(a) for a in ("gx", "gy", "gz")]).astype(jnp.int32)
     own = (BX, BY, BZ)
-    to_upper, to_lower = call(send_z, "send_z", (right_side, phase_mask), [own] * 2)
-    below, above = from_below(to_upper, "gz"), from_above(to_lower, "gz")
-    part = (2 * BX + 4, 8, Z0)
-    upper, lower = call(send_y, "send_y", (right_side, phase_mask, below, above), [part] * 2)
+    upper, lower = call(send_y, "send_y", (right_side, phase_mask), [(2 * BX + 4, 8, 128)] * 2)
     below, above = from_below(upper, "gy"), from_above(lower, "gy")
-    to_upper, to_lower = call(send_x, "send_x", (lower, upper, below, above), [(18, Y0, Z0)] * 2)
+    to_upper, to_lower = call(send_x, "send_x", (lower, upper, below, above), [(18, Y0, 128)] * 2)
     x_below, x_above = from_below(to_upper, "gx"), from_above(to_lower, "gx")
+    pieces = (lower, upper, below, above, x_below, x_above)
+    to_upper, to_lower = call(send_z, "send_z", pieces, [(51, Y0, 128)] * 2)
+    z_below, z_above = from_below(to_upper, "gz"), from_above(to_lower, "gz")
 
     full = (X0, Y0, Z0)
     *faces_0, r0, total, packed = call(
         functools.partial(begin, sizes), "begin",
-        (where, lower, upper, below, above, x_below, x_above),
+        (where, *pieces, z_below, z_above),
         [full] * 6 + [own, (64, 8, 128)],
         [(X0 + 2, Y0, Z0), (X0, Z0), (X0, Z0)] + [(X0, BY, Z0)] * 3 + [full] * 2,
     )
@@ -561,18 +631,17 @@
         rows = jnp.concatenate(parts, 1)
         below, above = from_below(rows, "gx"), from_above(rows, "gx")
         state = [full_1] * 2 + [full_2] * 2
-        planes = 16 if first else 4
         made = call(
             functools.partial(down, sizes, first), "down",
             (where, rows, below, above, *levels),
-            ([full_1] * 5 + [full_2] * 5 if first else []) + state + [(planes, 2 * ny, 128)],
+            ([full_1] * 5 + [full_2] * 5 if first else []) + state + [(4, 2 * ny, 128)],
             [full_1] * 2,
         )
         if first:
             levels, made = made[:10], made[10:]
         r1, e1, r2, e2, packed = made
         below, above = from_below(packed, "gz"), from_above(packed, "gz")
-        (copies,) = call(spread, "spread", (packed, below, above), [(nx,) + packed.shape])
+        (copies,) = call(spread, "spread", (packed, below, above), [(nx, 8 if first else 4, 2 * ny, 128)])
         gathered = lax.all_to_all(copies, "gx", 0, 0)
         args = (where, gathered, *level_3, *levels[5:], r2, e2, *levels[:5], r1, e1, *faces_0, r0, total)
         full_3 = (4 * nx, 2 * ny, 128)

time: 227 us -> 187 us (0.82)
  Pallas kernels: 74.5 us -> 45.5 us
  blocking collectives: 34.4 us -> 28.8 us
  waiting for transfers between devices: 85.7 us -> 80.3 us
    pallas_call x10, Pallas kernels: 74.5 us -> 45.5 us  [call(): pl.pallas_call(kernel, out_shape=[jax.ShapeDtypeStruct(s, F32) for s in o...]
    all_to_all x2, blocking collectives: 34.4 us -> 28.8 us  [body(): gathered = lax.all_to_all(copies, 'gx', 0, 0)]
    ppermute x13, waiting for transfers between devices: 57.3 us -> 53.1 us  [from_above(): return lax.ppermute(array, axis, [((i + by) % n, i) for i in range(n)])]
  transfers between devices with their start and end apart: 20 -> 20, of which waited for: 15 -> 14; matrix products, arithmetic and copies ran while one was open for 0% -> 0% of each run, Pallas kernels for 0% -> 0%
where the time goes in v1:
time: 187 us
  waiting for transfers between devices  80.3 us (43%)
  Pallas kernels  45.5 us (24%)
  blocking collectives  28.8 us (15%)
  starting transfers between devices  27.1 us (14%)
  local copies, waits for them, and re-layouts  4.4 us (2%)
    ppermute x13, waiting for transfers between devices, from_above(): return lax.ppermute(array, axis, [((i + by) % n, i) for i in range(n)])  53.1 us
    pallas_call x10, Pallas kernels, call(): pl.pallas_call(kernel, out_shape=[jax.ShapeDtypeStruct(s, F32) for s in o...  45.5 us
    all_to_all x2, blocking collectives, body(): gathered = lax.all_to_all(copies, 'gx', 0, 0)  28.8 us
    ppermute x7, waiting for transfers between devices, from_below(): return lax.ppermute(array, axis, [(i, (i + 1) % n) for i in range(n)])  27.2 us
    ppermute x13, starting transfers between devices, from_above(): return lax.ppermute(array, axis, [((i + by) % n, i) for i in range(n)])  20.1 us
    ppermute x7, starting transfers between devices, from_below(): return lax.ppermute(array, axis, [(i, (i + 1) % n) for i in range(n)])  6.94 us
    unnamed x24, local copies, waits for them, and re-layouts  4.37 us
  transfers between devices with their start and end apart: 20, of which 14 were waited for; matrix products, arithmetic and copies ran while one was open for 0% of the time, Pallas kernels for 0%

profile of v1, /device:TPU:6, one launch (start us, length us, event | category | flops | bytes accessed | tf_op | source)
XLA Modules:
  0.0 186.9 jit_solution(1845030301028535890)
XLA Ops:
  0.6 0.0 copy-start.7
  0.6 0.9 copy-done.7
  1.6 0.9 copy-done.8
  2.5 0.1 send_y.1
  2.6 0.9 collective-permute-start.1
  3.5 2.4 %collective-permute-start = (f32[68,8,128]{2,1,0:T(8,128)S(1)}, f32[68,8,128]{2,1,0:T(8,128)S(1)}, u32[]{:S(2)}, u32[]{:S(2)}) collective-permute-start(f32[68,8,128]{2,1,0:T(8,128)S(1)} %get-tuple-element.45.upper), channel_id=1, source_target_pairs={{0,8},{8,16},{16,24},{24,0},{1,9},{9,17},{17,25},{25,1},{2,10},{10... | collective-permute-start | bytes 835592 | tf_op jit(solution)/shard_map/ppermute | solution.py:596
  5.9 6.4 %collective-permute-done.1.above = f32[68,8,128]{2,1,0:T(8,128)S(1)} collective-permute-done((f32[68,8,128]{2,1,0:T(8,128)S(1)}, f32[68,8,128]{2,1,0:T(8,128)S(1)}, u32[]{:S(2)}, u32[]{:S(2)}) %collective-permute-start.1) | collective-permute-done | bytes 278560 | tf_op jit(solution)/shard_map/ppermute | solution.py:601
  12.3 0.0 collective-permute-done.below
  12.3 0.1 send_x.1
  12.3 2.0 %collective-permute-start.2 = (f32[18,32,128]{2,1,0:T(8,128)S(1)}, f32[18,32,128]{2,1,0:T(8,128)S(1)}, u32[]{:S(2)}, u32[]{:S(2)}) collective-permute-start(f32[18,32,128]{2,1,0:T(8,128)S(1)} %get-tuple-element.46), channel_id=1, source_target_pairs={{0,32},{32,64},{64,96},{96,128},{128,160},{160,192},{192,224},{224... | collective-permute-start | bytes 884744 | tf_op jit(solution)/shard_map/ppermute | solution.py:596
  14.3 4.0 %collective-permute-start.3 = (f32[18,32,128]{2,1,0:T(8,128)S(1)}, f32[18,32,128]{2,1,0:T(8,128)S(1)}, u32[]{:S(2)}, u32[]{:S(2)}) collective-permute-start(f32[18,32,128]{2,1,0:T(8,128)S(1)} %get-tuple-element.47), channel_id=1, source_target_pairs={{32,0},{64,32},{96,64},{128,96},{160,128},{192,160},{224,192},{0,2... | collective-permute-start | bytes 884744 | tf_op jit(solution)/shard_map/ppermute | solution.py:601
  18.4 6.0 %collective-permute-done.2.x_below = f32[18,32,128]{2,1,0:T(8,128)S(1)} collective-permute-done((f32[18,32,128]{2,1,0:T(8,128)S(1)}, f32[18,32,128]{2,1,0:T(8,128)S(1)}, u32[]{:S(2)}, u32[]{:S(2)}) %collective-permute-start.2) | collective-permute-done | bytes 294944 | tf_op jit(solution)/shard_map/ppermute | solution.py:596
  24.4 0.0 collective-permute-done.3.x_above
  24.4 1.6 send_z.1
  26.0 0.0 collective-permute-start.4
  26.1 3.0 %collective-permute-start.5 = (f32[51,32,128]{2,1,0:T(8,128)}, f32[51,32,128]{2,1,0:T(8,128)S(1)}, u32[]{:S(2)}, u32[]{:S(2)}) collective-permute-start(f32[51,32,128]{2,1,0:T(8,128)} %get-tuple-element.49), channel_id=1, source_target_pairs={{1,0},{2,1},{3,2},{4,3},{5,4},{6,5},{7,6},{0,7},{9,8},{10,9},{11,1... | collective-permute-start | bytes 2506760 | tf_op jit(solution)/shard_map/ppermute | solution.py:601
  29.0 0.1 pad_add_fusion.where
  29.1 10.3 %collective-permute-done.4.z_below = f32[51,32,128]{2,1,0:T(8,128)S(1)} collective-permute-done((f32[51,32,128]{2,1,0:T(8,128)}, f32[51,32,128]{2,1,0:T(8,128)S(1)}, u32[]{:S(2)}, u32[]{:S(2)}) %collective-permute-start.4) | collective-permute-done | bytes 835616 | tf_op jit(solution)/shard_map/ppermute | solution.py:596
  39.4 0.0 collective-permute-done.5.z_above
  39.4 9.4 %begin.1 = (f32[48,32,256]{2,1,0:T(8,128)S(1)}, f32[48,32,256]{2,1,0:T(8,128)S(1)}, f32[48,32,256]{2,1,0:T(8,128)S(1)}, f32[48,32,256]{2,1,0:T(8,128)S(1)}, f32[...) custom-call(s32[3]{0:T(128)S(1)} %pad_add_fusion.where, ...), custom_call_target="tpu_custom_call" | custom-call | tf_op jit(solution)/shard_map/begin/pallas_call | solution.py:582
  48.8 1.2 copy-done.4
  50.0 1.2 copy-done.5
  51.2 0.0 collective-permute-start.6
  51.2 4.1 %collective-permute-start.7 = (f32[64,8,128]{2,1,0:T(8,128)S(1)}, f32[64,8,128]{2,1,0:T(8,128)S(1)}, u32[]{:S(2)}, u32[]{:S(2)}) collective-permute-start(f32[64,8,128]{2,1,0:T(8,128)S(1)} %get-tuple-element.50), channel_id=1, source_target_pairs={{16,0},{24,8},{0,16},{8,24},{17,1},{25,9},{1,17},{9,25},{18,2},{26... | collective-permute-start | bytes 786440 | tf_op jit(solution)/shard_map/ppermute | solution.py:601
  55.3 0.0 collective-permute-start.8
  55.4 5.8 %collective-permute-done.6 = f32[64,8,128]{2,1,0:T(8,128)S(1)} collective-permute-done((f32[64,8,128]{2,1,0:T(8,128)S(1)}, f32[64,8,128]{2,1,0:T(8,128)S(1)}, u32[]{:S(2)}, u32[]{:S(2)}) %collective-permute-start.6) | collective-permute-done | bytes 262176 | tf_op jit(solution)/shard_map/ppermute | solution.py:601
  61.2 6.4 %collective-permute-done.7 = f32[64,8,128]{2,1,0:T(8,128)S(1)} collective-permute-done((f32[64,8,128]{2,1,0:T(8,128)S(1)}, f32[64,8,128]{2,1,0:T(8,128)S(1)}, u32[]{:S(2)}, u32[]{:S(2)}) %collective-permute-start.7) | collective-permute-done | bytes 262176 | tf_op jit(solution)/shard_map/ppermute | solution.py:601
  67.6 0.0 collective-permute-done.8
  67.7 3.1 %collective-permute-start.10 = (f32[64,32,128]{2,1,0:T(8,128)S(1)}, f32[64,32,128]{2,1,0:T(8,128)S(1)}, u32[]{:S(2)}, u32[]{:S(2)}) collective-permute-start(f32[64,32,128]{2,1,0:T(8,128)S(1)} %constant_dynamic-update-slice_fusion.own), channel_id=1, source_target_pairs={{32,0},{64,32},{96,64},{128,96},{160,128},{192,160},{224,192},{0,2... | collective-permute-start | bytes 3145736 | tf_op jit(solution)/shard_map/ppermute | solution.py:601
  70.8 0.0 collective-permute-start.9
  70.8 22.3 %collective-permute-done.10.above = f32[64,32,128]{2,1,0:T(8,128)S(1)} collective-permute-done((f32[64,32,128]{2,1,0:T(8,128)S(1)}, f32[64,32,128]{2,1,0:T(8,128)S(1)}, u32[]{:S(2)}, u32[]{:S(2)}) %collective-permute-start.10) | collective-permute-done | bytes 1048608 | tf_op jit(solution)/shard_map/ppermute | solution.py:601
  93.1 3.4 %collective-permute-done.9.below = f32[64,32,128]{2,1,0:T(8,128)S(1)} collective-permute-done((f32[64,32,128]{2,1,0:T(8,128)S(1)}, f32[64,32,128]{2,1,0:T(8,128)S(1)}, u32[]{:S(2)}, u32[]{:S(2)}) %collective-permute-start.9) | collective-permute-done | bytes 1048608 | tf_op jit(solution)/shard_map/ppermute | solution.py:596
  96.5 5.7 %down.2 = (f32[48,32,128]{2,1,0:T(8,128)S(1)}, f32[48,32,128]{2,1,0:T(8,128)S(1)}, f32[48,32,128]{2,1,0:T(8,128)S(1)}, f32[48,32,128]{2,1,0:T(8,128)S(1)}, f32[4...) custom-call(s32[3]{0:T(128)S(1)} %pad_add_fusion.where, ...), custom_call_target="tpu_custom_call" | custom-call | tf_op jit(solution)/shard_map/down/pallas_call | solution.py:582
  102.2 0.0 copy-done
  102.2 0.0 copy-done.2
  102.2 1.0 collective-permute-start.12
  103.2 0.0 collective-permute-start.11
  103.2 1.4 collective-permute-done.12.above
  104.7 2.9 %collective-permute-done.11.below = f32[4,8,128]{2,1,0:T(8,128)S(1)} collective-permute-done((f32[4,8,128]{2,1,0:T(8,128)S(1)}, f32[4,8,128]{2,1,0:T(8,128)S(1)}, u32[]{:S(2)}, u32[]{:S(2)}) %collective-permute-start.11) | collective-permute-done | bytes 16416 | tf_op jit(solution)/shard_map/ppermute | solution.py:596
  107.6 0.1 spread.2
  107.7 15.8 %all_to_all.10.gathered = f32[8,8,8,128]{3,2,1,0:T(8,128)S(1)} all-to-all(f32[8,8,8,128]{3,2,1,0:T(8,128)S(1)} %spread.2), channel_id=1, replica_groups=mesh['gx'=8,'gy'=4,'gz'=8] {'gx'}, dimensions={0} | all-to-all | bytes 524288 | tf_op jit(solution)/shard_map/all_to_all | solution.py:645
  123.5 14.7 %up.1 = (f32[32,8,128]{2,1,0:T(8,128)S(1)}, f32[32,8,128]{2,1,0:T(8,128)S(1)}, f32[32,8,128]{2,1,0:T(8,128)S(1)}, f32[32,8,128]{2,1,0:T(8,128)S(1)}, f32[32,8,12...) custom-call(s32[3]{0:T(128)S(1)} %pad_add_fusion.where, ...), custom_call_target="tpu_custom_call" | custom-call | tf_op jit(solution)/shard_map/up/pallas_call | solution.py:582
  138.2 0.0 copy-start.6
  138.2 3.0 %collective-permute-start.15 = (f32[16,8,128]{2,1,0:T(8,128)S(1)}, f32[16,8,128]{2,1,0:T(8,128)S(1)}, u32[]{:S(2)}, u32[]{:S(2)}) collective-permute-start(f32[16,8,128]{2,1,0:T(8,128)S(1)} %get-tuple-element.73), channel_id=1, source_target_pairs={{24,0},{0,8},{8,16},{16,24},{25,1},{1,9},{9,17},{17,25},{26,2},{2,... | collective-permute-start | bytes 196616 | tf_op jit(solution)/shard_map/ppermute | solution.py:601
  141.2 0.3 collective-permute-start.14
  141.4 0.7 collective-permute-start.13
  142.1 5.5 %collective-permute-done.13 = f32[16,8,128]{2,1,0:T(8,128)S(1)} collective-permute-done((f32[16,8,128]{2,1,0:T(8,128)S(1)}, f32[16,8,128]{2,1,0:T(8,128)S(1)}, u32[]{:S(2)}, u32[]{:S(2)}) %collective-permute-start.13) | collective-permute-done | bytes 65568 | tf_op jit(solution)/shard_map/ppermute | solution.py:601
  147.6 0.0 collective-permute-done.14
  147.6 0.0 collective-permute-done.15
  147.7 0.0 copy-start.1
  147.7 0.0 copy-start.3
  147.7 0.1 collective-permute-start.17
  147.8 2.0 %collective-permute-start.16 = (f32[16,32,128]{2,1,0:T(8,128)S(1)}, f32[16,32,128]{2,1,0:T(8,128)S(1)}, u32[]{:S(2)}, u32[]{:S(2)}) collective-permute-start(f32[16,32,128]{2,1,0:T(8,128)S(1)} %constant_dynamic-update-slice_fusion.4.own), channel_id=1, source_target_pairs={{0,32},{32,64},{64,96},{96,128},{128,160},{160,192},{192,224},{224... | collective-permute-start | bytes 786440 | tf_op jit(solution)/shard_map/ppermute | solution.py:596
  149.8 4.3 %collective-permute-done.17.above = f32[16,32,128]{2,1,0:T(8,128)S(1)} collective-permute-done((f32[16,32,128]{2,1,0:T(8,128)S(1)}, f32[16,32,128]{2,1,0:T(8,128)S(1)}, u32[]{:S(2)}, u32[]{:S(2)}) %collective-permute-start.17) | collective-permute-done | bytes 262176 | tf_op jit(solution)/shard_map/ppermute | solution.py:601
  154.1 1.5 collective-permute-done.16.below
  155.7 3.4 %down.3 = (f32[48,32,128]{2,1,0:T(8,128)S(1)}, f32[48,32,128]{2,1,0:T(8,128)S(1)}, f32[24,16,128]{2,1,0:T(8,128)S(1)}, f32[24,16,128]{2,1,0:T(8,128)S(1)}, f32[4,8,128]{2,1,0:T(8,128)S(1)}) custom-call(s32[3]{0:T(128)S(1)} %pad_add_fusion.where, f32[16,32,128]{2,1,0:T(8,128)S(1)} %constant_dynamic-update-slice_fusion.4.own, ...), custom_call_target="tpu_custom_call" | custom-call | tf_op jit(solution)/shard_map/down/pallas_call | solution.py:582
  159.1 0.0 collective-permute-start.19
  159.1 0.5 collective-permute-start.18
  159.6 0.9 collective-permute-done.19.above
  160.5 2.9 %collective-permute-done.18.below = f32[4,8,128]{2,1,0:T(8,128)S(1)} collective-permute-done((f32[4,8,128]{2,1,0:T(8,128)S(1)}, f32[4,8,128]{2,1,0:T(8,128)S(1)}, u32[]{:S(2)}, u32[]{:S(2)}) %collective-permute-start.18) | collective-permute-done | bytes 16416 | tf_op jit(solution)/shard_map/ppermute | solution.py:596
  163.5 0.1 spread.3
  163.5 13.1 %all_to_all.11.gathered = f32[8,4,8,128]{3,2,1,0:T(8,128)S(1)} all-to-all(f32[8,4,8,128]{3,2,1,0:T(8,128)S(1)} %spread.3), channel_id=1, replica_groups=mesh['gx'=8,'gy'=4,'gz'=8] {'gx'}, dimensions={0} | all-to-all | bytes 262144 | tf_op jit(solution)/shard_map/all_to_all | solution.py:645
  176.6 0.0 copy-done.3
  176.6 10.3 %up_last.1 = (f32[32,16,128]{2,1,0:T(8,128)}, f32[32,16,128]{2,1,0:T(8,128)}) custom-call(s32[3]{0:T(128)S(1)} %pad_add_fusion.where, f32[8,4,8,128]{3,2,1,0:T(8,128)S(1)} %all_to_all.11.gathered, f32[32,8,128]{2,1,0:T(8,128)S(1)} %get-tuple-element.75.refs_0_, f32[32,8,128]{2,1,0:T(8,128)S(1)} %get-tuple-element.76.refs_1_, ...), custom_call_target="tpu_custom_call" | custom-call | tf_op jit(solution)/shard_map/up_last/pallas_call | solution.py:582
  (15 shorter events, 0.1 us)
Async XLA Ops:
  0.6 1.0 copy-start.7
  1.6 0.9 copy-start.8
  2.6 9.7 %collective-permute-start.1 = (f32[68,8,128]{2,1,0:T(8,128)S(1)}, f32[68,8,128]{2,1,0:T(8,128)S(1)}, u32[]{:S(2)}, u32[]{:S(2)}) collective-permute-start(f32[68,8,128]{2,1,0:T(8,128)S(1)} %get-tuple-element.44.lower), channel_id=1, source_target_pairs={{8,0},{16,8},{24,16},{0,24},{9,1},{17,9},{25,17},{1,25},{10,2},{18... | collective-permute-start | bytes 835592 | tf_op jit(solution)/shard_map/ppermute | solution.py:601
  3.5 8.8 %collective-permute-start = (f32[68,8,128]{2,1,0:T(8,128)S(1)}, f32[68,8,128]{2,1,0:T(8,128)S(1)}, u32[]{:S(2)}, u32[]{:S(2)}) collective-permute-start(f32[68,8,128]{2,1,0:T(8,128)S(1)} %get-tuple-element.45.upper), channel_id=1, source_target_pairs={{0,8},{8,16},{16,24},{24,0},{1,9},{9,17},{17,25},{25,1},{2,10},{10... | collective-permute-start | bytes 835592 | tf_op jit(solution)/shard_map/ppermute | solution.py:596
  12.3 12.1 %collective-permute-start.2 = (f32[18,32,128]{2,1,0:T(8,128)S(1)}, f32[18,32,128]{2,1,0:T(8,128)S(1)}, u32[]{:S(2)}, u32[]{:S(2)}) collective-permute-start(f32[18,32,128]{2,1,0:T(8,128)S(1)} %get-tuple-element.46), channel_id=1, source_target_pairs={{0,32},{32,64},{64,96},{96,128},{128,160},{160,192},{192,224},{224... | collective-permute-start | bytes 884744 | tf_op jit(solution)/shard_map/ppermute | solution.py:596
  14.3 10.1 %collective-permute-start.3 = (f32[18,32,128]{2,1,0:T(8,128)S(1)}, f32[18,32,128]{2,1,0:T(8,128)S(1)}, u32[]{:S(2)}, u32[]{:S(2)}) collective-permute-start(f32[18,32,128]{2,1,0:T(8,128)S(1)} %get-tuple-element.47), channel_id=1, source_target_pairs={{32,0},{64,32},{96,64},{128,96},{160,128},{192,160},{224,192},{0,2... | collective-permute-start | bytes 884744 | tf_op jit(solution)/shard_map/ppermute | solution.py:601
  26.0 13.4 %collective-permute-start.4 = (f32[51,32,128]{2,1,0:T(8,128)}, f32[51,32,128]{2,1,0:T(8,128)S(1)}, u32[]{:S(2)}, u32[]{:S(2)}) collective-permute-start(f32[51,32,128]{2,1,0:T(8,128)} %get-tuple-element.48), channel_id=1, source_target_pairs={{0,1},{1,2},{2,3},{3,4},{4,5},{5,6},{6,7},{7,0},{8,9},{9,10},{10,1... | collective-permute-start | bytes 2506760 | tf_op jit(solution)/shard_map/ppermute | solution.py:596
  26.1 13.4 %collective-permute-start.5 = (f32[51,32,128]{2,1,0:T(8,128)}, f32[51,32,128]{2,1,0:T(8,128)S(1)}, u32[]{:S(2)}, u32[]{:S(2)}) collective-permute-start(f32[51,32,128]{2,1,0:T(8,128)} %get-tuple-element.49), channel_id=1, source_target_pairs={{1,0},{2,1},{3,2},{4,3},{5,4},{6,5},{7,6},{0,7},{9,8},{10,9},{11,1... | collective-permute-start | bytes 2506760 | tf_op jit(solution)/shard_map/ppermute | solution.py:601
  48.8 1.2 copy-start.4
  50.0 1.2 copy-start.5
  51.2 51.0 %copy-start = (f32[48,32,256]{2,1,0:T(8,128)}, f32[48,32,256]{2,1,0:T(8,128)S(1)}, u32[]{:S(2)}) copy-start(f32[48,32,256]{2,1,0:T(8,128)S(1)} %get-tuple-element.68.refs_16_.refs_21_) | copy-start | bytes 4718596
  51.2 51.0 %copy-start.2 = (f32[48,32,256]{2,1,0:T(8,128)}, f32[48,32,256]{2,1,0:T(8,128)S(1)}, u32[]{:S(2)}) copy-start(f32[48,32,256]{2,1,0:T(8,128)S(1)} %get-tuple-element.69.refs_17_.refs_22_) | copy-start | bytes 4718596
  51.2 9.9 %collective-permute-start.6 = (f32[64,8,128]{2,1,0:T(8,128)S(1)}, f32[64,8,128]{2,1,0:T(8,128)S(1)}, u32[]{:S(2)}, u32[]{:S(2)}) collective-permute-start(f32[64,8,128]{2,1,0:T(8,128)S(1)} %get-tuple-element.50), channel_id=1, source_target_pairs={{8,0},{16,8},{24,16},{0,24},{9,1},{17,9},{25,17},{1,25},{10,2},{18... | collective-permute-start | bytes 786440 | tf_op jit(solution)/shard_map/ppermute | solution.py:601
  51.2 16.4 %collective-permute-start.7 = (f32[64,8,128]{2,1,0:T(8,128)S(1)}, f32[64,8,128]{2,1,0:T(8,128)S(1)}, u32[]{:S(2)}, u32[]{:S(2)}) collective-permute-start(f32[64,8,128]{2,1,0:T(8,128)S(1)} %get-tuple-element.50), channel_id=1, source_target_pairs={{16,0},{24,8},{0,16},{8,24},{17,1},{25,9},{1,17},{9,25},{18,2},{26... | collective-permute-start | bytes 786440 | tf_op jit(solution)/shard_map/ppermute | solution.py:601
  55.3 12.3 %collective-permute-start.8 = (f32[64,8,128]{2,1,0:T(8,128)S(1)}, f32[64,8,128]{2,1,0:T(8,128)S(1)}, u32[]{:S(2)}, u32[]{:S(2)}) collective-permute-start(f32[64,8,128]{2,1,0:T(8,128)S(1)} %get-tuple-element.50), channel_id=1, source_target_pairs={{24,0},{0,8},{8,16},{16,24},{25,1},{1,9},{9,17},{17,25},{26,2},{2,... | collective-permute-start | bytes 786440 | tf_op jit(solution)/shard_map/ppermute | solution.py:601
  67.7 25.4 %collective-permute-start.10 = (f32[64,32,128]{2,1,0:T(8,128)S(1)}, f32[64,32,128]{2,1,0:T(8,128)S(1)}, u32[]{:S(2)}, u32[]{:S(2)}) collective-permute-start(f32[64,32,128]{2,1,0:T(8,128)S(1)} %constant_dynamic-update-slice_fusion.own), channel_id=1, source_target_pairs={{32,0},{64,32},{96,64},{128,96},{160,128},{192,160},{224,192},{0,2... | collective-permute-start | bytes 3145736 | tf_op jit(solution)/shard_map/ppermute | solution.py:601
  70.8 25.7 %collective-permute-start.9 = (f32[64,32,128]{2,1,0:T(8,128)S(1)}, f32[64,32,128]{2,1,0:T(8,128)S(1)}, u32[]{:S(2)}, u32[]{:S(2)}) collective-permute-start(f32[64,32,128]{2,1,0:T(8,128)S(1)} %constant_dynamic-update-slice_fusion.own), channel_id=1, source_target_pairs={{0,32},{32,64},{64,96},{96,128},{128,160},{160,192},{192,224},{224... | collective-permute-start | bytes 3145736 | tf_op jit(solution)/shard_map/ppermute | solution.py:596
  102.2 2.4 %collective-permute-start.12 = (f32[4,8,128]{2,1,0:T(8,128)S(1)}, f32[4,8,128]{2,1,0:T(8,128)S(1)}, u32[]{:S(2)}, u32[]{:S(2)}) collective-permute-start(f32[4,8,128]{2,1,0:T(8,128)S(1)} %get-tuple-element.51.own), channel_id=1, source_target_pairs={{1,0},{2,1},{3,2},{4,3},{5,4},{6,5},{7,6},{0,7},{9,8},{10,9},{11,1... | collective-permute-start | bytes 49160 | tf_op jit(solution)/shard_map/ppermute | solution.py:601
  103.2 4.4 %collective-permute-start.11 = (f32[4,8,128]{2,1,0:T(8,128)S(1)}, f32[4,8,128]{2,1,0:T(8,128)S(1)}, u32[]{:S(2)}, u32[]{:S(2)}) collective-permute-start(f32[4,8,128]{2,1,0:T(8,128)S(1)} %get-tuple-element.51.own), channel_id=1, source_target_pairs={{0,1},{1,2},{2,3},{3,4},{4,5},{5,6},{6,7},{7,0},{8,9},{9,10},{10,1... | collective-permute-start | bytes 49160 | tf_op jit(solution)/shard_map/ppermute | solution.py:596
  138.2 20.9 %copy-start.6 = (f32[48,32,256]{2,1,0:T(8,128)}, f32[48,32,256]{2,1,0:T(8,128)S(1)}, u32[]{:S(2)}) copy-start(f32[48,32,256]{2,1,0:T(8,128)S(1)} %get-tuple-element.84.refs_24_) | copy-start | bytes 4718596
  138.2 9.5 %collective-permute-start.15 = (f32[16,8,128]{2,1,0:T(8,128)S(1)}, f32[16,8,128]{2,1,0:T(8,128)S(1)}, u32[]{:S(2)}, u32[]{:S(2)}) collective-permute-start(f32[16,8,128]{2,1,0:T(8,128)S(1)} %get-tuple-element.73), channel_id=1, source_target_pairs={{24,0},{0,8},{8,16},{16,24},{25,1},{1,9},{9,17},{17,25},{26,2},{2,... | collective-permute-start | bytes 196616 | tf_op jit(solution)/shard_map/ppermute | solution.py:601
  141.2 6.5 %collective-permute-start.14 = (f32[16,8,128]{2,1,0:T(8,128)S(1)}, f32[16,8,128]{2,1,0:T(8,128)S(1)}, u32[]{:S(2)}, u32[]{:S(2)}) collective-permute-start(f32[16,8,128]{2,1,0:T(8,128)S(1)} %get-tuple-element.73), channel_id=1, source_target_pairs={{16,0},{24,8},{0,16},{8,24},{17,1},{25,9},{1,17},{9,25},{18,2},{26... | collective-permute-start | bytes 196616 | tf_op jit(solution)/shard_map/ppermute | solution.py:601
  141.4 6.2 %collective-permute-start.13 = (f32[16,8,128]{2,1,0:T(8,128)S(1)}, f32[16,8,128]{2,1,0:T(8,128)S(1)}, u32[]{:S(2)}, u32[]{:S(2)}) collective-permute-start(f32[16,8,128]{2,1,0:T(8,128)S(1)} %get-tuple-element.73), channel_id=1, source_target_pairs={{8,0},{16,8},{24,16},{0,24},{9,1},{17,9},{25,17},{1,25},{10,2},{18... | collective-permute-start | bytes 196616 | tf_op jit(solution)/shard_map/ppermute | solution.py:601
  147.7 29.0 %copy-start.1 = (f32[48,32,256]{2,1,0:T(8,128)S(1)}, f32[48,32,256]{2,1,0:T(8,128)}, u32[]{:S(2)}) copy-start(f32[48,32,256]{2,1,0:T(8,128)} %copy-done) | copy-start | bytes 4718596
  147.7 28.9 %copy-start.3 = (f32[48,32,256]{2,1,0:T(8,128)S(1)}, f32[48,32,256]{2,1,0:T(8,128)}, u32[]{:S(2)}) copy-start(f32[48,32,256]{2,1,0:T(8,128)} %copy-done.2) | copy-start | bytes 4718596
  147.7 6.5 %collective-permute-start.17 = (f32[16,32,128]{2,1,0:T(8,128)S(1)}, f32[16,32,128]{2,1,0:T(8,128)S(1)}, u32[]{:S(2)}, u32[]{:S(2)}) collective-permute-start(f32[16,32,128]{2,1,0:T(8,128)S(1)} %constant_dynamic-update-slice_fusion.4.own), channel_id=1, source_target_pairs={{32,0},{64,32},{96,64},{128,96},{160,128},{192,160},{224,192},{0,2... | collective-permute-start | bytes 786440 | tf_op jit(solution)/shard_map/ppermute | solution.py:601
  147.8 7.9 %collective-permute-start.16 = (f32[16,32,128]{2,1,0:T(8,128)S(1)}, f32[16,32,128]{2,1,0:T(8,128)S(1)}, u32[]{:S(2)}, u32[]{:S(2)}) collective-permute-start(f32[16,32,128]{2,1,0:T(8,128)S(1)} %constant_dynamic-update-slice_fusion.4.own), channel_id=1, source_target_pairs={{0,32},{32,64},{64,96},{96,128},{128,160},{160,192},{192,224},{224... | collective-permute-start | bytes 786440 | tf_op jit(solution)/shard_map/ppermute | solution.py:596
  159.1 1.5 collective-permute-start.19
  159.1 4.4 %collective-permute-start.18 = (f32[4,8,128]{2,1,0:T(8,128)S(1)}, f32[4,8,128]{2,1,0:T(8,128)S(1)}, u32[]{:S(2)}, u32[]{:S(2)}) collective-permute-start(f32[4,8,128]{2,1,0:T(8,128)S(1)} %get-tuple-element.74.own), channel_id=1, source_target_pairs={{0,1},{1,2},{2,3},{3,4},{4,5},{5,6},{6,7},{7,0},{8,9},{9,10},{10,1... | collective-permute-start | bytes 49160 | tf_op jit(solution)/shard_map/ppermute | solution.py:596

commit v2 on v1

--- a/solution.py
+++ b/solution.py
@@ -15,7 +15,7 @@
 GAS = 1.0
 
 INTERPRET = False
-VMEM_LIMIT = 40 * 1024 * 1024
+VMEM_LIMIT = 28 * 1024 * 1024
 
 BX, BY, BZ = 32, 16, 128
 WX = 8
@@ -215,7 +215,7 @@
         out[50, 16:32] = jnp.zeros((16, 128), F32)
 
 
-def presmooth_0(where, r, faces, inv, d0, d1, start, stop, have_first):
+def presmooth_0(r, faces, inv, d0, d1, start, stop, have_first):
     if not have_first:
         def first(at, n):
             here = pl.ds(at, n)
@@ -257,19 +257,22 @@
     return jnp.where(total < 5.0, 1.0, jnp.where(total < 15.0, 2.0 / 11.0, 0.1))
 
 
-def begin(sizes, where, lower, upper, below, above, x_below, x_above, z_below, z_above,
-          fx, fy, fz, diag, inv, r, total, packed, rho, low, up, raw_x, raw_y, raw_z, d0, d1):
+def sides(below, above, at):
+    one, two = above[at], below[at]
+    axis = one.ndim - 1
+    lane = iota(one.shape, axis)
+    return jnp.where(lane < 64, one, two), roll(jnp.where(lane >= 64, one, two), 64, axis)
+
+
+def faces_0(sizes, where, lower, upper, below, above, x_below, x_above, z_below, z_above,
+            fx, fy, fz, diag, inv, packed, rho, low, up, raw_x, raw_y, raw_z):
     nx, ny, nz = sizes
     gx0, gy0, gz0 = where[0] * BX, where[1] * BY, where[2] * BZ
     own, side = slice(0, 128), slice(128, 256)
-    r[0:8, :, own] = x_below[0:8]
-    r[40:48, :, own] = x_above[0:8]
     rho[0:9, :, own] = x_below[8:17]
     rho[41:50, :, own] = x_above[8:17]
     for tile, source in enumerate((lower, upper, above, below)):
-        rows = slice(8 * tile, 8 * tile + 8)
-        r[8:40, rows, own] = source[0:BX]
-        rho[9:41, rows, own] = source[BX : 2 * BX]
+        rho[9:41, 8 * tile : 8 * tile + 8, own] = source[BX : 2 * BX]
     low[0:8, own] = x_below[17, 0:8]
     up[0:8, own] = x_below[17, 8:16]
     low[40:48, own] = x_above[17, 0:8]
@@ -278,19 +281,13 @@
         low[8 + 8 * n : 16 + 8 * n, own] = below[2 * BX + n]
         up[8 + 8 * n : 16 + 8 * n, own] = above[2 * BX + n]
 
-    def sides(at):
-        one, two = z_above[at], z_below[at]
-        axis = one.ndim - 1
-        lane = iota(one.shape, axis)
-        return jnp.where(lane < 64, one, two), roll(jnp.where(lane >= 64, one, two), 64, axis)
-
     def side_planes(p, n):
-        r[pl.ds(p, n), :, side], rho[pl.ds(p + 1, n), :, side] = sides(pl.ds(p, n))
+        rho[pl.ds(p + 1, n), :, side] = sides(z_below, z_above, pl.ds(p, n))[1]
 
     loop(0, X0, 4, side_planes)
-    rho[0, :, side], rho[49, :, side] = sides(48)
-    low[0:32, side], up[0:32, side] = sides(49)
-    low_rest, up_rest = sides(50)
+    rho[0, :, side], rho[49, :, side] = sides(z_below, z_above, 48)
+    low[0:32, side], up[0:32, side] = sides(z_below, z_above, 49)
+    low_rest, up_rest = sides(z_below, z_above, 50)
     low[32:48, side], up[32:48, side] = low_rest[0:16], up_rest[0:16]
 
     def plane(p, n):
@@ -312,7 +309,6 @@
         i = 1.0 / d
         diag[p] = d
         inv[p] = i
-        d0[p] = (FIRST * r[p]) * i
         raw_x[p] = f_x[0:16]
         raw_y[p] = f_y[0:16]
         raw_z[p] = f_z[0:16]
@@ -321,10 +317,6 @@
         fz[p] = jnp.where((gz == nz - 1) | (gz == -1), 0.0, f_z)
 
     loop(0, X0, 1, plane, UC)
-    faces = (fx, fy, fz, diag)
-    presmooth_0(where, r, faces, inv, d0, d1, 0, X0, True)
-    add_own(total, (d0, d1), True)
-    restrict_0(r, packed.at[0:16])
     lanes, odd_lanes = lane_pairs(256, 0.125), lane_pairs(256, 0.125, True)
     for n, (raw, rows, columns) in enumerate((
         (raw_x, row_pairs(16, odd_x=True), lanes),
@@ -333,7 +325,26 @@
     )):
         for g in range(4):
             block = raw[WX + 8 * g : WX + 8 * g + 8]
-            packed[16 * (n + 1) + 4 * g : 16 * (n + 1) + 4 * g + 4] = coarsen(block, rows, columns)
+            packed[16 * n + 4 * g : 16 * n + 4 * g + 4] = coarsen(block, rows, columns)
+
+
+def begin(lower, upper, below, above, x_below, x_above, z_below, z_above, fx, fy, fz, diag, inv,
+          r, total, packed, d0, d1):
+    own, side = slice(0, 128), slice(128, 256)
+    r[0:8, :, own] = x_below[0:8]
+    r[40:48, :, own] = x_above[0:8]
+    for tile, source in enumerate((lower, upper, above, below)):
+        r[8:40, 8 * tile : 8 * tile + 8, own] = source[0:BX]
+
+    def first(p, n):
+        here = pl.ds(p, n)
+        r[here, :, side] = sides(z_below, z_above, here)[0]
+        d0[here] = (FIRST * r[here]) * inv[here]
+
+    loop(0, X0, B0, first, U0)
+    presmooth_0(r, (fx, fy, fz, diag), inv, d0, d1, 0, X0, True)
+    add_own(total, (d0, d1), True)
+    restrict_0(r, packed)
 
 
 def assemble_1(part, own, below, above, out):
@@ -352,69 +363,70 @@
     loop(start, stop, B1, second)
 
 
-def down(sizes, first, where, own, below, above, *refs):
+def faces_1(sizes, where, own, below, above,
+            fx, fy, fz, diag, inv, gx2, gy2, gz2, diag2, inv2, packed):
     n1 = tuple(n // 2 for n in sizes)
     n2 = tuple(n // 4 for n in sizes)
-    if first:
-        (fx, fy, fz, diag, inv, gx2, gy2, gz2, diag2, inv2, r, e, r2_out, e2_out, packed, d0, d1) = refs
-    else:
-        (fx, fy, fz, diag, inv, gx2, gy2, gz2, diag2, inv2, r, e, r2_out, e2_out, packed, d0, d1) = refs
+    ny1 = fx.shape[1]
+    ny2 = ny1 // 2
+    rows, lanes, odd_lanes = row_pairs(ny1), lane_pairs(128, 0.125), lane_pairs(128, 0.125, True)
+    coarse = []
+    for n, (raw, rows_matrix, columns) in enumerate((
+        (fx, row_pairs(ny1, odd_x=True), lanes),
+        (fy, row_pairs(ny1, odd_y=True), lanes),
+        (fz, rows, odd_lanes),
+    )):
+        assemble_1(slice(16 * n, 16 * (n + 1)), own, below, above, raw)
+        coarse.append(jnp.concatenate(
+            [coarsen(raw[8 * g : 8 * g + 8], rows_matrix, columns) for g in range(6)], 0))
+    shape = (B1, ny1, 128)
+    gy = lax.rem(where[1] * 8 + iota(shape, 1), n1[1])
+    lane = iota(shape, 2)
+    gz = where[2] * 64 + jnp.where(lane < 96, lane, lane - 128)
+
+    def planes(n, count):
+        at = X1 - B1 - n
+        here = pl.ds(at, B1)
+        gx = where[0] * 16 + at - 16 + iota(shape, 0)
+        c = fx[here]
+        before = jnp.concatenate([fx[pl.ds(jnp.maximum(at - 1, 0), 1)], c[:-1]], 0)
+        level = level_of(c, before, fy[here], fz[here], gx, gy, gz, n1)
+        fx[here], fy[here], fz[here], diag[here], inv[here] = level
+
+    loop(0, X1, B1, planes)
+    shape = (X2, ny2, 128)
+    lane = iota(shape, 2)
+    at_2 = (
+        where[0] * 8 - 8 + iota(shape, 0),
+        lax.rem(where[1] * 4 + iota(shape, 1), n2[1]),
+        where[2] * 32 + jnp.where(lane < 64, lane, lane - 128),
+    )
+    level_2 = level_of(coarse[0], step_x(coarse[0], 1), coarse[1], coarse[2], *at_2, n2)
+    gx2[...], gy2[...], gz2[...], diag2[...], inv2[...] = level_2
+    sent = None
+    for n, (rows_matrix, columns) in enumerate((
+        (row_pairs(ny2, odd_x=True), lanes),
+        (row_pairs(ny2, odd_y=True), lanes),
+        (row_pairs(ny2), odd_lanes),
+    )):
+        at = 16 * (n + 1)
+        value = roll(coarsen(coarse[n][8:16], rows_matrix, columns), at, 2)
+        sent = value if sent is None else jnp.where(iota(value.shape, 2) < at, sent, value)
+    packed[...] = sent
+
+
+def down(own, below, above, fx, fy, fz, diag, inv, gx2, gy2, gz2, diag2, inv2, *refs):
+    *given, r, e, r2_out, e2_out, packed, d0, d1 = refs
     ny1 = fx.shape[1]
     ny2 = ny1 // 2
     assemble_1(slice(0, 16), own, below, above, r)
     rows, lanes = row_pairs(ny1), lane_pairs(128, 0.125)
-    if first:
-        raws = (fx, fy, fz)
-        for n, raw in enumerate(raws):
-            assemble_1(slice(16 * (n + 1), 16 * (n + 2)), own, below, above, raw)
-        odd_lanes = lane_pairs(128, 0.125, True)
-        coarse = []
-        for raw, rows_matrix, columns in (
-            (fx, row_pairs(ny1, odd_x=True), lanes),
-            (fy, row_pairs(ny1, odd_y=True), lanes),
-            (fz, rows, odd_lanes),
-        ):
-            coarse.append(jnp.concatenate(
-                [coarsen(raw[8 * g : 8 * g + 8], rows_matrix, columns) for g in range(6)], 0))
-        shape = (B1, ny1, 128)
-        gy = lax.rem(where[1] * 8 + iota(shape, 1), n1[1])
-        lane = iota(shape, 2)
-        gz = where[2] * 64 + jnp.where(lane < 96, lane, lane - 128)
-
-        def planes(n, count):
-            at = X1 - B1 - n
-            here = pl.ds(at, B1)
-            gx = where[0] * 16 + at - 16 + iota(shape, 0)
-            c = fx[here]
-            before = jnp.concatenate([fx[pl.ds(jnp.maximum(at - 1, 0), 1)], c[:-1]], 0)
-            level = level_of(c, before, fy[here], fz[here], gx, gy, gz, n1)
-            fx[here], fy[here], fz[here], diag[here], inv[here] = level
-            d0[here] = (FIRST * r[here]) * level[4]
-
-        loop(0, X1, B1, planes)
-        shape = (X2, ny2, 128)
-        lane = iota(shape, 2)
-        at_2 = (
-            where[0] * 8 - 8 + iota(shape, 0),
-            lax.rem(where[1] * 4 + iota(shape, 1), n2[1]),
-            where[2] * 32 + jnp.where(lane < 64, lane, lane - 128),
-        )
-        raw_2 = tuple(coarse)
-        level_2 = level_of(raw_2[0], step_x(raw_2[0], 1), raw_2[1], raw_2[2], *at_2, n2)
-        gx2[...], gy2[...], gz2[...], diag2[...], inv2[...] = level_2
-        for n, (rows_matrix, columns) in enumerate((
-            (row_pairs(ny2, odd_x=True), lanes),
-            (row_pairs(ny2, odd_y=True), lanes),
-            (row_pairs(ny2), odd_lanes),
-        )):
-            coarse[n] = coarsen(raw_2[n][8:16], rows_matrix, columns)
-    else:
-        def begin_1(at, n):
-            here = pl.ds(at, n)
-            d0[here] = (FIRST * r[here]) * inv[here]
-
-        loop(0, X1, B1, begin_1)
-
+
+    def begin_1(at, n):
+        here = pl.ds(at, n)
+        d0[here] = (FIRST * r[here]) * inv[here]
+
+    loop(0, X1, B1, begin_1)
     faces = (fx, fy, fz, diag)
     relax_1(r, faces, inv, d0, d1, 1, X1 - 1)
 
@@ -435,11 +447,8 @@
     r2_out[...] = r2
     e2_out[...] = d + d_next
     sent = coarsen(r2[8:16], row_pairs(ny2), lanes)
-    if first:
-        lane = iota(sent.shape, 2)
-        for n in range(3):
-            at = 16 * (n + 1)
-            sent = jnp.where(lane < at, sent, roll(coarse[n], at, 2))
+    if given:
+        sent = jnp.where(iota(sent.shape, 2) < 16, sent, given[0][...])
     packed[...] = sent
 
 
@@ -563,7 +572,7 @@
         d0[here] = (FIRST * left) * inv[here]
 
     loop(begin_at, end_at, B0, lift_0, U0)
-    presmooth_0(where, r, faces, inv, d0, d1, begin_at, end_at, True)
+    presmooth_0(r, faces, inv, d0, d1, begin_at, end_at, True)
     if last:
         pressure[...] = total_in[...]
         add_own(pressure, (p0, d0, d1), False)
@@ -571,12 +580,12 @@
         return
     total[...] = total_in[...]
     add_own(total, (p0, d0, d1), False)
-    presmooth_0(where, r, faces, inv, d0, d1, 4, 44, False)
+    presmooth_0(r, faces, inv, d0, d1, 4, 44, False)
     add_own(total, (d0, d1), False)
     restrict_0(r, packed)
 
 
-def call(kernel, name, args, outs, scratch=()):
+def call(kernel, name, args, outs, scratch=(), us=0):
     vmem = pl.BlockSpec(memory_space=pltpu.VMEM)
     smem = pl.BlockSpec(memory_space=pltpu.SMEM)
     return pl.pallas_call(
@@ -587,6 +596,7 @@
         scratch_shapes=[pltpu.VMEM(s, F32) for s in scratch],
         compiler_params=pltpu.CompilerParams(vmem_limit_bytes=VMEM_LIMIT),
         name=name,
+        cost_estimate=pl.CostEstimate(flops=0, bytes_accessed=us * 3_500_000, transcendentals=0) if us else None,
         interpret=INTERPRET,
     )(*args)
 
@@ -615,43 +625,43 @@
     z_below, z_above = from_below(to_upper, "gz"), from_above(to_lower, "gz")
 
     full = (X0, Y0, Z0)
-    *faces_0, r0, total, packed = call(
-        functools.partial(begin, sizes), "begin",
-        (where, *pieces, z_below, z_above),
-        [full] * 6 + [own, (64, 8, 128)],
-        [(X0 + 2, Y0, Z0), (X0, Z0), (X0, Z0)] + [(X0, BY, Z0)] * 3 + [full] * 2,
-    )
     full_1 = (X1, 8 * ny, 128)
     full_2 = (X2, 4 * ny, 128)
-    levels = []
+    full_3 = (4 * nx, 2 * ny, 128)
+
+    def around(packed):
+        parts = [packed] + [from_above(packed, "gy", s) for s in range(1, ny)]
+        rows = jnp.concatenate(parts, 1)
+        return rows, from_below(rows, "gx"), from_above(rows, "gx")
+
+    *level_0, packed = call(
+        functools.partial(faces_0, sizes), "faces_0", (where, *pieces, z_below, z_above),
+        [full] * 5 + [(48, 8, 128)],
+        [(X0 + 2, Y0, Z0), (X0, Z0), (X0, Z0)] + [(X0, BY, Z0)] * 3, us=5,
+    )
+    around_faces = around(packed)
+    r0, total, packed = call(
+        begin, "begin", (*pieces, z_below, z_above, *level_0), [full, own, (16, 8, 128)], [full] * 2, us=6)
+    *levels, faces_3 = call(
+        functools.partial(faces_1, sizes), "faces_1", (where, *around_faces),
+        [full_1] * 5 + [full_2] * 5 + [(4, 2 * ny, 128)], us=3)
     level_3 = []
     for cycle in range(2):
         first = cycle == 0
-        parts = [packed] + [from_above(packed, "gy", s) for s in range(1, ny)]
-        rows = jnp.concatenate(parts, 1)
-        below, above = from_below(rows, "gx"), from_above(rows, "gx")
-        state = [full_1] * 2 + [full_2] * 2
-        made = call(
-            functools.partial(down, sizes, first), "down",
-            (where, rows, below, above, *levels),
-            ([full_1] * 5 + [full_2] * 5 if first else []) + state + [(4, 2 * ny, 128)],
-            [full_1] * 2,
-        )
-        if first:
-            levels, made = made[:10], made[10:]
-        r1, e1, r2, e2, packed = made
+        r1, e1, r2, e2, packed = call(
+            down, "down", (*around(packed), *levels, *([faces_3] if first else [])),
+            [full_1] * 2 + [full_2] * 2 + [(4, 2 * ny, 128)], [full_1] * 2, us=4)
         below, above = from_below(packed, "gz"), from_above(packed, "gz")
         (copies,) = call(spread, "spread", (packed, below, above), [(nx, 8 if first else 4, 2 * ny, 128)])
         gathered = lax.all_to_all(copies, "gx", 0, 0)
-        args = (where, gathered, *level_3, *levels[5:], r2, e2, *levels[:5], r1, e1, *faces_0, r0, total)
-        full_3 = (4 * nx, 2 * ny, 128)
+        args = (where, gathered, *level_3, *levels[5:], r2, e2, *levels[:5], r1, e1, *level_0, r0, total)
         scratch = [full_3] + [full_1] * 4 + [(X1, 16, 128)] + [full] * 3
         if first:
             *level_3, r0, total, packed = call(
                 functools.partial(up, sizes, False), "up", args,
-                [full_3] * 5 + [full, own, (16, 8, 128)], scratch)
+                [full_3] * 5 + [full, own, (16, 8, 128)], scratch, us=15)
         else:
-            return tuple(call(functools.partial(up, sizes, True), "up_last", args, [own] * 2, [full] + scratch))
+            return tuple(call(functools.partial(up, sizes, True), "up_last", args, [own] * 2, [full] + scratch, us=10))
 
 
 def solution(mesh):

time: 187 us -> 171 us (0.914)
  waiting for transfers between devices: 80.3 us -> 63.2 us
  starting transfers between devices: 27.1 us -> 33.5 us
  Pallas kernels: 45.5 us -> 42.3 us
  local copies, waits for them, and re-layouts: 4.4 us -> 2 us
    ppermute x13 -> x17, waiting for transfers between devices: 53.1 us -> 34.9 us  [from_above(): return lax.ppermute(array, axis, [((i + by) % n, i) for i in range(n)])]
    ppermute x13 -> x17, starting transfers between devices: 20.1 us -> 26.6 us  [from_above(): return lax.ppermute(array, axis, [((i + by) % n, i) for i in range(n)])]
    pallas_call x10 -> x12, Pallas kernels: 45.5 us -> 42.3 us  [call(): pl.pallas_call(kernel, out_shape=[jax.ShapeDtypeStruct(s, F32) for s in o...]
    unnamed x24 -> x13, local copies, waits for them, and re-layouts: 4.37 us -> 1.97 us
    ppermute x7 -> x8, waiting for transfers between devices: 27.2 us -> 28.3 us  [from_below(): return lax.ppermute(array, axis, [(i, (i + 1) % n) for i in range(n)])]
    ppermute x7 -> x8, starting transfers between devices: 6.94 us -> 6.94 us  [from_below(): return lax.ppermute(array, axis, [(i, (i + 1) % n) for i in range(n)])]
  transfers between devices with their start and end apart: 20 -> 25, of which waited for: 14 -> 16; matrix products, arithmetic and copies ran while one was open for 0% -> 0% of each run, Pallas kernels for 0% -> 4%
where the time goes in v2:
time: 171 us
  waiting for transfers between devices  63.2 us (37%)
  Pallas kernels  42.3 us (25%)
  starting transfers between devices  33.5 us (20%)
  blocking collectives  29.1 us (17%)
  local copies, waits for them, and re-layouts  2 us (1%)
    pallas_call x12, Pallas kernels, call(): pl.pallas_call(kernel, out_shape=[jax.ShapeDtypeStruct(s, F32) for s in o...  42.3 us
    ppermute x17, waiting for transfers between devices, from_above(): return lax.ppermute(array, axis, [((i + by) % n, i) for i in range(n)])  34.9 us
    all_to_all x2, blocking collectives, body(): gathered = lax.all_to_all(copies, 'gx', 0, 0)  29.1 us
    ppermute x8, waiting for transfers between devices, from_below(): return lax.ppermute(array, axis, [(i, (i + 1) % n) for i in range(n)])  28.3 us
    ppermute x17, starting transfers between devices, from_above(): return lax.ppermute(array, axis, [((i + by) % n, i) for i in range(n)])  26.6 us
    ppermute x8, starting transfers between devices, from_below(): return lax.ppermute(array, axis, [(i, (i + 1) % n) for i in range(n)])  6.94 us
  transfers between devices with their start and end apart: 25, of which 16 were waited for; matrix products, arithmetic and copies ran while one was open for 0% of the time, Pallas kernels for 4%

profile of v2, /device:TPU:6, one launch (start us, length us, event | category | flops | bytes accessed | tf_op | source)
XLA Modules:
  0.0 171.0 jit_solution(13330144893352188218)
XLA Ops:
  0.6 0.9 copy-done
  1.6 0.9 copy-done.1
  2.5 0.1 send_y.1
  2.6 0.9 collective-permute-start.1
  3.5 2.4 %collective-permute-start = (f32[68,8,128]{2,1,0:T(8,128)S(1)}, f32[68,8,128]{2,1,0:T(8,128)S(1)}, u32[]{:S(2)}, u32[]{:S(2)}) collective-permute-start(f32[68,8,128]{2,1,0:T(8,128)S(1)} %get-tuple-element.47.upper), channel_id=1, source_target_pairs={{0,8},{8,16},{16,24},{24,0},{1,9},{9,17},{17,25},{25,1},{2,10},{10... | collective-permute-start | bytes 835592 | tf_op jit(solution)/shard_map/ppermute | solution.py:606
  5.9 6.4 %collective-permute-done.1.above = f32[68,8,128]{2,1,0:T(8,128)S(1)} collective-permute-done((f32[68,8,128]{2,1,0:T(8,128)S(1)}, f32[68,8,128]{2,1,0:T(8,128)S(1)}, u32[]{:S(2)}, u32[]{:S(2)}) %collective-permute-start.1) | collective-permute-done | bytes 278560 | tf_op jit(solution)/shard_map/ppermute | solution.py:611
  12.3 0.0 collective-permute-done.below
  12.3 0.1 send_x.1
  12.3 2.0 %collective-permute-start.2 = (f32[18,32,128]{2,1,0:T(8,128)S(1)}, f32[18,32,128]{2,1,0:T(8,128)S(1)}, u32[]{:S(2)}, u32[]{:S(2)}) collective-permute-start(f32[18,32,128]{2,1,0:T(8,128)S(1)} %get-tuple-element.48), channel_id=1, source_target_pairs={{0,32},{32,64},{64,96},{96,128},{128,160},{160,192},{192,224},{224... | collective-permute-start | bytes 884744 | tf_op jit(solution)/shard_map/ppermute | solution.py:606
  14.3 4.0 %collective-permute-start.3 = (f32[18,32,128]{2,1,0:T(8,128)S(1)}, f32[18,32,128]{2,1,0:T(8,128)S(1)}, u32[]{:S(2)}, u32[]{:S(2)}) collective-permute-start(f32[18,32,128]{2,1,0:T(8,128)S(1)} %get-tuple-element.49), channel_id=1, source_target_pairs={{32,0},{64,32},{96,64},{128,96},{160,128},{192,160},{224,192},{0,2... | collective-permute-start | bytes 884744 | tf_op jit(solution)/shard_map/ppermute | solution.py:611
  18.4 6.0 %collective-permute-done.2.x_below = f32[18,32,128]{2,1,0:T(8,128)S(1)} collective-permute-done((f32[18,32,128]{2,1,0:T(8,128)S(1)}, f32[18,32,128]{2,1,0:T(8,128)S(1)}, u32[]{:S(2)}, u32[]{:S(2)}) %collective-permute-start.2) | collective-permute-done | bytes 294944 | tf_op jit(solution)/shard_map/ppermute | solution.py:606
  24.4 0.0 collective-permute-done.3.x_above
  24.4 1.6 send_z.1
  26.1 0.0 collective-permute-start.4
  26.1 3.0 %collective-permute-start.5 = (f32[51,32,128]{2,1,0:T(8,128)}, f32[51,32,128]{2,1,0:T(8,128)S(1)}, u32[]{:S(2)}, u32[]{:S(2)}) collective-permute-start(f32[51,32,128]{2,1,0:T(8,128)} %get-tuple-element.51), channel_id=1, source_target_pairs={{1,0},{2,1},{3,2},{4,3},{5,4},{6,5},{7,6},{0,7},{9,8},{10,9},{11,1... | collective-permute-start | bytes 2506760 | tf_op jit(solution)/shard_map/ppermute | solution.py:611
  29.0 0.1 pad_add_fusion.where
  29.1 10.3 %collective-permute-done.4.z_below = f32[51,32,128]{2,1,0:T(8,128)S(1)} collective-permute-done((f32[51,32,128]{2,1,0:T(8,128)}, f32[51,32,128]{2,1,0:T(8,128)S(1)}, u32[]{:S(2)}, u32[]{:S(2)}) %collective-permute-start.4) | collective-permute-done | bytes 835616 | tf_op jit(solution)/shard_map/ppermute | solution.py:606
  39.4 0.0 collective-permute-done.5.z_above
  39.4 5.5 %faces_0.1 = (f32[48,32,256]{2,1,0:T(8,128)S(1)}, f32[48,32,256]{2,1,0:T(8,128)S(1)}, f32[48,32,256]{2,1,0:T(8,128)S(1)}, f32[48,32,256]{2,1,0:T(8,128)S(1)}, f3...) custom-call(s32[3]{0:T(128)S(1)} %pad_add_fusion.where, f32[68,8,128]{2,1,0:T(8,128)S(1)} %get-tuple-element.46.lower, ...), custom_call_target="tpu_custom_call" | custom-call | bytes 17500000 | tf_op jit(solution)/shard_map/faces_0/pallas_call | solution.py:591
  44.9 0.1 collective-permute-start.11
  45.0 3.2 %collective-permute-start.13 = (f32[48,8,128]{2,1,0:T(8,128)S(1)}, f32[48,8,128]{2,1,0:T(8,128)S(1)}, u32[]{:S(2)}, u32[]{:S(2)}) collective-permute-start(f32[48,8,128]{2,1,0:T(8,128)S(1)} %get-tuple-element.58), channel_id=1, source_target_pairs={{24,0},{0,8},{8,16},{16,24},{25,1},{1,9},{9,17},{17,25},{26,2},{2,... | collective-permute-start | bytes 589832 | tf_op jit(solution)/shard_map/ppermute | solution.py:611
  48.2 0.9 collective-permute-start.12
  49.1 4.4 %collective-permute-done.11 = f32[48,8,128]{2,1,0:T(8,128)S(1)} collective-permute-done((f32[48,8,128]{2,1,0:T(8,128)S(1)}, f32[48,8,128]{2,1,0:T(8,128)S(1)}, u32[]{:S(2)}, u32[]{:S(2)}) %collective-permute-start.11) | collective-permute-done | bytes 196640 | tf_op jit(solution)/shard_map/ppermute | solution.py:611
  53.5 5.1 %collective-permute-done.12 = f32[48,8,128]{2,1,0:T(8,128)S(1)} collective-permute-done((f32[48,8,128]{2,1,0:T(8,128)S(1)}, f32[48,8,128]{2,1,0:T(8,128)S(1)}, u32[]{:S(2)}, u32[]{:S(2)}) %collective-permute-start.12) | collective-permute-done | bytes 196640 | tf_op jit(solution)/shard_map/ppermute | solution.py:611
  58.6 3.1 %collective-permute-start.15 = (f32[48,32,128]{2,1,0:T(8,128)S(1)}, f32[48,32,128]{2,1,0:T(8,128)S(1)}, u32[]{:S(2)}, u32[]{:S(2)}) collective-permute-start(f32[48,32,128]{2,1,0:T(8,128)S(1)} %constant_dynamic-update-slice_fusion.4.own), channel_id=1, source_target_pairs={{32,0},{64,32},{96,64},{128,96},{160,128},{192,160},{224,192},{0,2... | collective-permute-start | bytes 2359304 | tf_op jit(solution)/shard_map/ppermute | solution.py:611
  61.7 0.0 collective-permute-start.14
  61.7 4.2 %begin.1 = (f32[48,32,256]{2,1,0:T(8,128)S(1)}, f32[32,16,128]{2,1,0:T(8,128)S(1)}, f32[16,8,128]{2,1,0:T(8,128)S(1)}) custom-call(f32[68,8,128]{2,1,0:T(8,128)S(1)} %get-tuple-element.46.lower, f32[68,8,128]{2,1,0:T(8,128)S(1)} %get-tuple-element.47.upper, f32[68,8,128]{2,1,0:T(8,128)S(1)} %collective-permute-done.below, ...), custom_call_target="tpu_custom_call" | custom-call | bytes 21000000 | tf_op jit(solution)/shard_map/begin/pallas_call | solution.py:591
  65.9 2.1 %collective-permute-start.8 = (f32[16,8,128]{2,1,0:T(8,128)S(1)}, f32[16,8,128]{2,1,0:T(8,128)S(1)}, u32[]{:S(2)}, u32[]{:S(2)}) collective-permute-start(f32[16,8,128]{2,1,0:T(8,128)S(1)} %get-tuple-element.57), channel_id=1, source_target_pairs={{24,0},{0,8},{8,16},{16,24},{25,1},{1,9},{9,17},{17,25},{26,2},{2,... | collective-permute-start | bytes 196616 | tf_op jit(solution)/shard_map/ppermute | solution.py:611
  68.1 1.1 collective-permute-start.7
  69.2 0.0 collective-permute-start.6
  69.2 5.5 %collective-permute-done.6 = f32[16,8,128]{2,1,0:T(8,128)S(1)} collective-permute-done((f32[16,8,128]{2,1,0:T(8,128)S(1)}, f32[16,8,128]{2,1,0:T(8,128)S(1)}, u32[]{:S(2)}, u32[]{:S(2)}) %collective-permute-start.6) | collective-permute-done | bytes 65568 | tf_op jit(solution)/shard_map/ppermute | solution.py:611
  74.7 0.0 collective-permute-done.7
  74.7 0.0 collective-permute-done.8
  74.8 3.5 %collective-permute-start.10 = (f32[16,32,128]{2,1,0:T(8,128)S(1)}, f32[16,32,128]{2,1,0:T(8,128)S(1)}, u32[]{:S(2)}, u32[]{:S(2)}) collective-permute-start(f32[16,32,128]{2,1,0:T(8,128)S(1)} %constant_dynamic-update-slice_fusion.own), channel_id=1, source_target_pairs={{32,0},{64,32},{96,64},{128,96},{160,128},{192,160},{224,192},{0,2... | collective-permute-start | bytes 786440 | tf_op jit(solution)/shard_map/ppermute | solution.py:611
  78.3 1.4 collective-permute-done.15.above
  79.7 3.7 %collective-permute-done.14.below = f32[48,32,128]{2,1,0:T(8,128)S(1)} collective-permute-done((f32[48,32,128]{2,1,0:T(8,128)S(1)}, f32[48,32,128]{2,1,0:T(8,128)S(1)}, u32[]{:S(2)}, u32[]{:S(2)}) %collective-permute-start.14) | collective-permute-done | bytes 786464 | tf_op jit(solution)/shard_map/ppermute | solution.py:606
  83.4 2.9 %faces_1.1 = (f32[48,32,128]{2,1,0:T(8,128)S(1)}, f32[48,32,128]{2,1,0:T(8,128)S(1)}, f32[48,32,128]{2,1,0:T(8,128)S(1)}, f32[48,32,128]{2,1,0:T(8,128)S(1)}, f3...) custom-call(s32[3]{0:T(128)S(1)} %pad_add_fusion.where, ...), custom_call_target="tpu_custom_call" | custom-call | bytes 10500000 | tf_op jit(solution)/shard_map/faces_1/pallas_call | solution.py:591
  86.3 0.0 collective-permute-done.10.above
  86.3 1.1 collective-permute-done.9.below
  87.4 2.9 %down.2 = (f32[48,32,128]{2,1,0:T(8,128)S(1)}, f32[48,32,128]{2,1,0:T(8,128)S(1)}, f32[24,16,128]{2,1,0:T(8,128)S(1)}, f32[24,16,128]{2,1,0:T(8,128)S(1)}, f32[4,8,128]{2,1,0:T(8,128)S(1)}) custom-call(f32[16,32,128]{2,1,0:T(8,128)S(1)} %constant_dynamic-update-slice_fusion.own, f32[16,32,128]{2,1,0:T(8,128)S(1)} %collective-permute-done.9.below, ...), custom_call_target="tpu_custom_call" | custom-call | bytes 14000000 | tf_op jit(solution)/shard_map/down/pallas_call | solution.py:591
  90.3 1.0 collective-permute-start.17
  91.2 0.0 collective-permute-start.16
  91.2 1.4 collective-permute-done.17.above
  92.7 2.9 %collective-permute-done.16.below = f32[4,8,128]{2,1,0:T(8,128)S(1)} collective-permute-done((f32[4,8,128]{2,1,0:T(8,128)S(1)}, f32[4,8,128]{2,1,0:T(8,128)S(1)}, u32[]{:S(2)}, u32[]{:S(2)}) %collective-permute-start.16) | collective-permute-done | bytes 16416 | tf_op jit(solution)/shard_map/ppermute | solution.py:606
  95.6 0.1 spread.2
  95.7 15.8 %all_to_all.10.gathered = f32[8,8,8,128]{3,2,1,0:T(8,128)S(1)} all-to-all(f32[8,8,8,128]{3,2,1,0:T(8,128)S(1)} %spread.2), channel_id=1, replica_groups=mesh['gx'=8,'gy'=4,'gz'=8] {'gx'}, dimensions={0} | all-to-all | bytes 524288 | tf_op jit(solution)/shard_map/all_to_all | solution.py:656
  111.5 12.9 %up.1 = (f32[32,8,128]{2,1,0:T(8,128)S(1)}, f32[32,8,128]{2,1,0:T(8,128)S(1)}, f32[32,8,128]{2,1,0:T(8,128)S(1)}, f32[32,8,128]{2,1,0:T(8,128)S(1)}, f32[32,8,12...) custom-call(s32[3]{0:T(128)S(1)} %pad_add_fusion.where, ...), custom_call_target="tpu_custom_call" | custom-call | bytes 52500000 | tf_op jit(solution)/shard_map/up/pallas_call | solution.py:591
  124.4 2.4 %collective-permute-start.20 = (f32[16,8,128]{2,1,0:T(8,128)S(1)}, f32[16,8,128]{2,1,0:T(8,128)S(1)}, u32[]{:S(2)}, u32[]{:S(2)}) collective-permute-start(f32[16,8,128]{2,1,0:T(8,128)S(1)} %get-tuple-element.77), channel_id=1, source_target_pairs={{24,0},{0,8},{8,16},{16,24},{25,1},{1,9},{9,17},{17,25},{26,2},{2,... | collective-permute-start | bytes 196616 | tf_op jit(solution)/shard_map/ppermute | solution.py:611
  126.8 1.1 collective-permute-start.19
  127.9 0.0 collective-permute-start.18
  128.0 5.5 %collective-permute-done.18 = f32[16,8,128]{2,1,0:T(8,128)S(1)} collective-permute-done((f32[16,8,128]{2,1,0:T(8,128)S(1)}, f32[16,8,128]{2,1,0:T(8,128)S(1)}, u32[]{:S(2)}, u32[]{:S(2)}) %collective-permute-start.18) | collective-permute-done | bytes 65568 | tf_op jit(solution)/shard_map/ppermute | solution.py:611
  133.4 0.0 collective-permute-done.19
  133.4 0.0 collective-permute-done.20
  133.5 0.1 collective-permute-start.22
  133.6 2.0 %collective-permute-start.21 = (f32[16,32,128]{2,1,0:T(8,128)S(1)}, f32[16,32,128]{2,1,0:T(8,128)S(1)}, u32[]{:S(2)}, u32[]{:S(2)}) collective-permute-start(f32[16,32,128]{2,1,0:T(8,128)S(1)} %constant_dynamic-update-slice_fusion.8.own), channel_id=1, source_target_pairs={{0,32},{32,64},{64,96},{96,128},{128,160},{160,192},{192,224},{224... | collective-permute-start | bytes 786440 | tf_op jit(solution)/shard_map/ppermute | solution.py:606
  135.6 4.3 %collective-permute-done.22.above = f32[16,32,128]{2,1,0:T(8,128)S(1)} collective-permute-done((f32[16,32,128]{2,1,0:T(8,128)S(1)}, f32[16,32,128]{2,1,0:T(8,128)S(1)}, u32[]{:S(2)}, u32[]{:S(2)}) %collective-permute-start.22) | collective-permute-done | bytes 262176 | tf_op jit(solution)/shard_map/ppermute | solution.py:611
  139.9 1.3 collective-permute-done.21.below
  141.2 2.9 %down.3 = (f32[48,32,128]{2,1,0:T(8,128)S(1)}, f32[48,32,128]{2,1,0:T(8,128)S(1)}, f32[24,16,128]{2,1,0:T(8,128)S(1)}, f32[24,16,128]{2,1,0:T(8,128)S(1)}, f32[4,8,128]{2,1,0:T(8,128)S(1)}) custom-call(f32[16,32,128]{2,1,0:T(8,128)S(1)} %constant_dynamic-update-slice_fusion.8.own, f32[16,32,128]{2,1,0:T(8,128)S(1)} %collective-permute-done.21.below, ...), custom_call_target="tpu_custom_call" | custom-call | bytes 14000000 | tf_op jit(solution)/shard_map/down/pallas_call | solution.py:591
  144.1 0.5 collective-permute-start.23
  144.6 0.9 collective-permute-done.24.above
  145.6 2.9 %collective-permute-done.23.below = f32[4,8,128]{2,1,0:T(8,128)S(1)} collective-permute-done((f32[4,8,128]{2,1,0:T(8,128)S(1)}, f32[4,8,128]{2,1,0:T(8,128)S(1)}, u32[]{:S(2)}, u32[]{:S(2)}) %collective-permute-start.23) | collective-permute-done | bytes 16416 | tf_op jit(solution)/shard_map/ppermute | solution.py:606
  148.5 0.1 spread.3
  148.6 13.3 %all_to_all.11.gathered = f32[8,4,8,128]{3,2,1,0:T(8,128)S(1)} all-to-all(f32[8,4,8,128]{3,2,1,0:T(8,128)S(1)} %spread.3), channel_id=1, replica_groups=mesh['gx'=8,'gy'=4,'gz'=8] {'gx'}, dimensions={0} | all-to-all | bytes 262144 | tf_op jit(solution)/shard_map/all_to_all | solution.py:656
  161.9 9.1 %up_last.1 = (f32[32,16,128]{2,1,0:T(8,128)}, f32[32,16,128]{2,1,0:T(8,128)}) custom-call(s32[3]{0:T(128)S(1)} %pad_add_fusion.where, f32[8,4,8,128]{3,2,1,0:T(8,128)S(1)} %all_to_all.11.gathered, f32[32,8,128]{2,1,0:T(8,128)S(1)} %get-tuple-element.79.refs_0_, f32[32,8,128]{2,1,0:T(8,128)S(1)} %get-tuple-element.80.refs_1_, ...), custom_call_target="tpu_custom_call" | custom-call | bytes 35000000 | tf_op jit(solution)/shard_map/up_last/pallas_call | solution.py:591
  (17 shorter events, 0.1 us)
Async XLA Ops:
  0.6 1.0 copy-start
  1.6 0.9 copy-start.1
  2.6 9.7 %collective-permute-start.1 = (f32[68,8,128]{2,1,0:T(8,128)S(1)}, f32[68,8,128]{2,1,0:T(8,128)S(1)}, u32[]{:S(2)}, u32[]{:S(2)}) collective-permute-start(f32[68,8,128]{2,1,0:T(8,128)S(1)} %get-tuple-element.46.lower), channel_id=1, source_target_pairs={{8,0},{16,8},{24,16},{0,24},{9,1},{17,9},{25,17},{1,25},{10,2},{18... | collective-permute-start | bytes 835592 | tf_op jit(solution)/shard_map/ppermute | solution.py:611
  3.5 8.8 %collective-permute-start = (f32[68,8,128]{2,1,0:T(8,128)S(1)}, f32[68,8,128]{2,1,0:T(8,128)S(1)}, u32[]{:S(2)}, u32[]{:S(2)}) collective-permute-start(f32[68,8,128]{2,1,0:T(8,128)S(1)} %get-tuple-element.47.upper), channel_id=1, source_target_pairs={{0,8},{8,16},{16,24},{24,0},{1,9},{9,17},{17,25},{25,1},{2,10},{10... | collective-permute-start | bytes 835592 | tf_op jit(solution)/shard_map/ppermute | solution.py:606
  12.3 12.1 %collective-permute-start.2 = (f32[18,32,128]{2,1,0:T(8,128)S(1)}, f32[18,32,128]{2,1,0:T(8,128)S(1)}, u32[]{:S(2)}, u32[]{:S(2)}) collective-permute-start(f32[18,32,128]{2,1,0:T(8,128)S(1)} %get-tuple-element.48), channel_id=1, source_target_pairs={{0,32},{32,64},{64,96},{96,128},{128,160},{160,192},{192,224},{224... | collective-permute-start | bytes 884744 | tf_op jit(solution)/shard_map/ppermute | solution.py:606
  14.3 10.1 %collective-permute-start.3 = (f32[18,32,128]{2,1,0:T(8,128)S(1)}, f32[18,32,128]{2,1,0:T(8,128)S(1)}, u32[]{:S(2)}, u32[]{:S(2)}) collective-permute-start(f32[18,32,128]{2,1,0:T(8,128)S(1)} %get-tuple-element.49), channel_id=1, source_target_pairs={{32,0},{64,32},{96,64},{128,96},{160,128},{192,160},{224,192},{0,2... | collective-permute-start | bytes 884744 | tf_op jit(solution)/shard_map/ppermute | solution.py:611
  26.1 13.4 %collective-permute-start.4 = (f32[51,32,128]{2,1,0:T(8,128)}, f32[51,32,128]{2,1,0:T(8,128)S(1)}, u32[]{:S(2)}, u32[]{:S(2)}) collective-permute-start(f32[51,32,128]{2,1,0:T(8,128)} %get-tuple-element.50), channel_id=1, source_target_pairs={{0,1},{1,2},{2,3},{3,4},{4,5},{5,6},{6,7},{7,0},{8,9},{9,10},{10,1... | collective-permute-start | bytes 2506760 | tf_op jit(solution)/shard_map/ppermute | solution.py:606
  26.1 13.4 %collective-permute-start.5 = (f32[51,32,128]{2,1,0:T(8,128)}, f32[51,32,128]{2,1,0:T(8,128)S(1)}, u32[]{:S(2)}, u32[]{:S(2)}) collective-permute-start(f32[51,32,128]{2,1,0:T(8,128)} %get-tuple-element.51), channel_id=1, source_target_pairs={{1,0},{2,1},{3,2},{4,3},{5,4},{6,5},{7,6},{0,7},{9,8},{10,9},{11,1... | collective-permute-start | bytes 2506760 | tf_op jit(solution)/shard_map/ppermute | solution.py:611
  44.9 8.6 %collective-permute-start.11 = (f32[48,8,128]{2,1,0:T(8,128)S(1)}, f32[48,8,128]{2,1,0:T(8,128)S(1)}, u32[]{:S(2)}, u32[]{:S(2)}) collective-permute-start(f32[48,8,128]{2,1,0:T(8,128)S(1)} %get-tuple-element.58), channel_id=1, source_target_pairs={{8,0},{16,8},{24,16},{0,24},{9,1},{17,9},{25,17},{1,25},{10,2},{18... | collective-permute-start | bytes 589832 | tf_op jit(solution)/shard_map/ppermute | solution.py:611
  45.0 13.6 %collective-permute-start.13 = (f32[48,8,128]{2,1,0:T(8,128)S(1)}, f32[48,8,128]{2,1,0:T(8,128)S(1)}, u32[]{:S(2)}, u32[]{:S(2)}) collective-permute-start(f32[48,8,128]{2,1,0:T(8,128)S(1)} %get-tuple-element.58), channel_id=1, source_target_pairs={{24,0},{0,8},{8,16},{16,24},{25,1},{1,9},{9,17},{17,25},{26,2},{2,... | collective-permute-start | bytes 589832 | tf_op jit(solution)/shard_map/ppermute | solution.py:611
  48.2 10.3 %collective-permute-start.12 = (f32[48,8,128]{2,1,0:T(8,128)S(1)}, f32[48,8,128]{2,1,0:T(8,128)S(1)}, u32[]{:S(2)}, u32[]{:S(2)}) collective-permute-start(f32[48,8,128]{2,1,0:T(8,128)S(1)} %get-tuple-element.58), channel_id=1, source_target_pairs={{16,0},{24,8},{0,16},{8,24},{17,1},{25,9},{1,17},{9,25},{18,2},{26... | collective-permute-start | bytes 589832 | tf_op jit(solution)/shard_map/ppermute | solution.py:611
  58.6 21.1 %collective-permute-start.15 = (f32[48,32,128]{2,1,0:T(8,128)S(1)}, f32[48,32,128]{2,1,0:T(8,128)S(1)}, u32[]{:S(2)}, u32[]{:S(2)}) collective-permute-start(f32[48,32,128]{2,1,0:T(8,128)S(1)} %constant_dynamic-update-slice_fusion.4.own), channel_id=1, source_target_pairs={{32,0},{64,32},{96,64},{128,96},{160,128},{192,160},{224,192},{0,2... | collective-permute-start | bytes 2359304 | tf_op jit(solution)/shard_map/ppermute | solution.py:611
  61.7 21.7 %collective-permute-start.14 = (f32[48,32,128]{2,1,0:T(8,128)S(1)}, f32[48,32,128]{2,1,0:T(8,128)S(1)}, u32[]{:S(2)}, u32[]{:S(2)}) collective-permute-start(f32[48,32,128]{2,1,0:T(8,128)S(1)} %constant_dynamic-update-slice_fusion.4.own), channel_id=1, source_target_pairs={{0,32},{32,64},{64,96},{96,128},{128,160},{160,192},{192,224},{224... | collective-permute-start | bytes 2359304 | tf_op jit(solution)/shard_map/ppermute | solution.py:606
  65.9 8.8 %collective-permute-start.8 = (f32[16,8,128]{2,1,0:T(8,128)S(1)}, f32[16,8,128]{2,1,0:T(8,128)S(1)}, u32[]{:S(2)}, u32[]{:S(2)}) collective-permute-start(f32[16,8,128]{2,1,0:T(8,128)S(1)} %get-tuple-element.57), channel_id=1, source_target_pairs={{24,0},{0,8},{8,16},{16,24},{25,1},{1,9},{9,17},{17,25},{26,2},{2,... | collective-permute-start | bytes 196616 | tf_op jit(solution)/shard_map/ppermute | solution.py:611
  68.1 6.6 %collective-permute-start.7 = (f32[16,8,128]{2,1,0:T(8,128)S(1)}, f32[16,8,128]{2,1,0:T(8,128)S(1)}, u32[]{:S(2)}, u32[]{:S(2)}) collective-permute-start(f32[16,8,128]{2,1,0:T(8,128)S(1)} %get-tuple-element.57), channel_id=1, source_target_pairs={{16,0},{24,8},{0,16},{8,24},{17,1},{25,9},{1,17},{9,25},{18,2},{26... | collective-permute-start | bytes 196616 | tf_op jit(solution)/shard_map/ppermute | solution.py:611
  69.2 5.5 %collective-permute-start.6 = (f32[16,8,128]{2,1,0:T(8,128)S(1)}, f32[16,8,128]{2,1,0:T(8,128)S(1)}, u32[]{:S(2)}, u32[]{:S(2)}) collective-permute-start(f32[16,8,128]{2,1,0:T(8,128)S(1)} %get-tuple-element.57), channel_id=1, source_target_pairs={{8,0},{16,8},{24,16},{0,24},{9,1},{17,9},{25,17},{1,25},{10,2},{18... | collective-permute-start | bytes 196616 | tf_op jit(solution)/shard_map/ppermute | solution.py:611
  74.8 11.6 %collective-permute-start.10 = (f32[16,32,128]{2,1,0:T(8,128)S(1)}, f32[16,32,128]{2,1,0:T(8,128)S(1)}, u32[]{:S(2)}, u32[]{:S(2)}) collective-permute-start(f32[16,32,128]{2,1,0:T(8,128)S(1)} %constant_dynamic-update-slice_fusion.own), channel_id=1, source_target_pairs={{32,0},{64,32},{96,64},{128,96},{160,128},{192,160},{224,192},{0,2... | collective-permute-start | bytes 786440 | tf_op jit(solution)/shard_map/ppermute | solution.py:611
  78.2 9.1 %collective-permute-start.9 = (f32[16,32,128]{2,1,0:T(8,128)S(1)}, f32[16,32,128]{2,1,0:T(8,128)S(1)}, u32[]{:S(2)}, u32[]{:S(2)}) collective-permute-start(f32[16,32,128]{2,1,0:T(8,128)S(1)} %constant_dynamic-update-slice_fusion.own), channel_id=1, source_target_pairs={{0,32},{32,64},{64,96},{96,128},{128,160},{160,192},{192,224},{224... | collective-permute-start | bytes 786440 | tf_op jit(solution)/shard_map/ppermute | solution.py:606
  90.3 2.4 %collective-permute-start.17 = (f32[4,8,128]{2,1,0:T(8,128)S(1)}, f32[4,8,128]{2,1,0:T(8,128)S(1)}, u32[]{:S(2)}, u32[]{:S(2)}) collective-permute-start(f32[4,8,128]{2,1,0:T(8,128)S(1)} %get-tuple-element.70.own), channel_id=1, source_target_pairs={{1,0},{2,1},{3,2},{4,3},{5,4},{6,5},{7,6},{0,7},{9,8},{10,9},{11,1... | collective-permute-start | bytes 49160 | tf_op jit(solution)/shard_map/ppermute | solution.py:611
  91.2 4.4 %collective-permute-start.16 = (f32[4,8,128]{2,1,0:T(8,128)S(1)}, f32[4,8,128]{2,1,0:T(8,128)S(1)}, u32[]{:S(2)}, u32[]{:S(2)}) collective-permute-start(f32[4,8,128]{2,1,0:T(8,128)S(1)} %get-tuple-element.70.own), channel_id=1, source_target_pairs={{0,1},{1,2},{2,3},{3,4},{4,5},{5,6},{6,7},{7,0},{8,9},{9,10},{10,1... | collective-permute-start | bytes 49160 | tf_op jit(solution)/shard_map/ppermute | solution.py:606
  124.4 9.1 %collective-permute-start.20 = (f32[16,8,128]{2,1,0:T(8,128)S(1)}, f32[16,8,128]{2,1,0:T(8,128)S(1)}, u32[]{:S(2)}, u32[]{:S(2)}) collective-permute-start(f32[16,8,128]{2,1,0:T(8,128)S(1)} %get-tuple-element.77), channel_id=1, source_target_pairs={{24,0},{0,8},{8,16},{16,24},{25,1},{1,9},{9,17},{17,25},{26,2},{2,... | collective-permute-start | bytes 196616 | tf_op jit(solution)/shard_map/ppermute | solution.py:611
  126.8 6.6 %collective-permute-start.19 = (f32[16,8,128]{2,1,0:T(8,128)S(1)}, f32[16,8,128]{2,1,0:T(8,128)S(1)}, u32[]{:S(2)}, u32[]{:S(2)}) collective-permute-start(f32[16,8,128]{2,1,0:T(8,128)S(1)} %get-tuple-element.77), channel_id=1, source_target_pairs={{16,0},{24,8},{0,16},{8,24},{17,1},{25,9},{1,17},{9,25},{18,2},{26... | collective-permute-start | bytes 196616 | tf_op jit(solution)/shard_map/ppermute | solution.py:611
  127.9 5.5 %collective-permute-start.18 = (f32[16,8,128]{2,1,0:T(8,128)S(1)}, f32[16,8,128]{2,1,0:T(8,128)S(1)}, u32[]{:S(2)}, u32[]{:S(2)}) collective-permute-start(f32[16,8,128]{2,1,0:T(8,128)S(1)} %get-tuple-element.77), channel_id=1, source_target_pairs={{8,0},{16,8},{24,16},{0,24},{9,1},{17,9},{25,17},{1,25},{10,2},{18... | collective-permute-start | bytes 196616 | tf_op jit(solution)/shard_map/ppermute | solution.py:611
  133.5 6.5 %collective-permute-start.22 = (f32[16,32,128]{2,1,0:T(8,128)S(1)}, f32[16,32,128]{2,1,0:T(8,128)S(1)}, u32[]{:S(2)}, u32[]{:S(2)}) collective-permute-start(f32[16,32,128]{2,1,0:T(8,128)S(1)} %constant_dynamic-update-slice_fusion.8.own), channel_id=1, source_target_pairs={{32,0},{64,32},{96,64},{128,96},{160,128},{192,160},{224,192},{0,2... | collective-permute-start | bytes 786440 | tf_op jit(solution)/shard_map/ppermute | solution.py:611
  133.6 7.7 %collective-permute-start.21 = (f32[16,32,128]{2,1,0:T(8,128)S(1)}, f32[16,32,128]{2,1,0:T(8,128)S(1)}, u32[]{:S(2)}, u32[]{:S(2)}) collective-permute-start(f32[16,32,128]{2,1,0:T(8,128)S(1)} %constant_dynamic-update-slice_fusion.8.own), channel_id=1, source_target_pairs={{0,32},{32,64},{64,96},{96,128},{128,160},{160,192},{192,224},{224... | collective-permute-start | bytes 786440 | tf_op jit(solution)/shard_map/ppermute | solution.py:606
  144.1 1.5 collective-permute-start.24
  144.1 4.4 %collective-permute-start.23 = (f32[4,8,128]{2,1,0:T(8,128)S(1)}, f32[4,8,128]{2,1,0:T(8,128)S(1)}, u32[]{:S(2)}, u32[]{:S(2)}) collective-permute-start(f32[4,8,128]{2,1,0:T(8,128)S(1)} %get-tuple-element.78.own), channel_id=1, source_target_pairs={{0,1},{1,2},{2,3},{3,4},{4,5},{5,6},{6,7},{7,0},{8,9},{9,10},{10,1... | collective-permute-start | bytes 49160 | tf_op jit(solution)/shard_map/ppermute | solution.py:606
